TPU v7x, 256 devices: a whole 4x4x8 slice. The times are simulated.
256 devices in a mesh: grp: 8 (over z_lo, core), dev: 32 (over y, z_hi, x).
Axes of the slice: x: 4, y: 4, z: 8 (z_hi: 2, z_lo: 4; z = z_hi * 4 + z_lo), core: 2. Of those that a mesh axis runs over, the one named last changes fastest.
Arguments:
- voltages: bfloat16 [2048, 268288], P(('grp', 'dev')), may hold values from -6 to 6
- weights: bfloat16 [512, 2, 512, 2048], P('dev', None, None, 'grp'), may hold values from -0.125 to 0.125
- input_map: int32 [2048], P('grp'), may hold values from 0 to 255, as said below
- beam_order: int32 [512], replicated, may hold values from 0 to 511, each once
Outputs:
- beam_power: float32 [512, 16, 512], P('dev', None, 'grp')
Inputs may be any that keep to these rules, and one draw needn't show every extreme that they name: `input_map`: each aligned block of 256 entries holds every number below 256 once. `beam_order`: each beam appears once.
All inputs are finite; a program needn't handle non-finite values.
Results may differ from a plain program's by a relative error of at most 0.0022.
Values may be sent and summed in bfloat16 or wider, within the bound.
No kernel may reach another device: no remote copies, remote signals or barrier semaphores. Data moves between devices by JAX's collectives and lax.ppermute only.
A program may use at most 128 MiB of HBM per device.

v0:
```python
import math

import jax
import jax.numpy as jnp
from jax import lax
from jax.sharding import PartitionSpec as P

CHAN = 1024
TAPS = 4
UPCH = 16
WIN = 512
SPECTRA = 128
BAND_LO = 256


def taper_table(nfft, tap_count):
    index = jnp.arange(tap_count * nfft, dtype=jnp.float32)
    centred = (index - tap_count * nfft / 2.0 + 0.5) / nfft
    window = 0.5 - 0.5 * jnp.cos(2.0 * math.pi * (index + 0.5) / (tap_count * nfft))
    return (jnp.sinc(centred) * window).reshape(tap_count, nfft)


def transform_table(chan, first, count):
    nfft = 2 * chan
    sample_ids = jnp.arange(nfft, dtype=jnp.int32)
    chan_ids = first + jnp.arange(count, dtype=jnp.int32)
    phases = chan_ids[:, None] * sample_ids[None, :] % nfft
    angles = 2.0 * math.pi * phases.astype(jnp.float32) / nfft
    factor = 1.0 / math.sqrt(chan)
    stacked = jnp.stack([jnp.cos(angles) * factor, -jnp.sin(angles) * factor], axis=1)
    return stacked.reshape(2 * count, nfft).astype(jnp.bfloat16)


def channelize(volts, chan, first, count, tap_count, spectra):
    nfft = 2 * chan
    frames = volts.astype(jnp.float32).reshape(volts.shape[0], spectra + tap_count - 1, nfft)
    taper = taper_table(nfft, tap_count)
    summed = taper[0] * frames[:, 0:spectra, :]
    for tap_index in range(1, tap_count):
        summed = summed + taper[tap_index] * frames[:, tap_index : tap_index + spectra, :]
    summed = summed.astype(jnp.bfloat16)
    return jnp.einsum(
        "kn,isn->ksi",
        transform_table(chan, first, count),
        summed,
        preferred_element_type=jnp.float32,
    ).astype(jnp.bfloat16)


def detect(beams, upch):
    blocks = beams.shape[3] // upch
    split_beams = beams.reshape(beams.shape[0], beams.shape[1], 2, blocks, upch)
    sub_ids = jnp.arange(upch, dtype=jnp.int32)
    phases = sub_ids[:, None] * sub_ids[None, :] % upch
    angles = 2.0 * math.pi * phases.astype(jnp.float32) / upch
    real_table = jnp.cos(angles) / math.sqrt(upch)
    imag_table = -jnp.sin(angles) / math.sqrt(upch)
    real_in = split_beams[:, :, 0]
    imag_in = split_beams[:, :, 1]
    highest = lax.Precision.HIGHEST
    real_out = jnp.einsum("ut,bckt->bcku", real_table, real_in, precision=highest) - jnp.einsum(
        "ut,bckt->bcku", imag_table, imag_in, precision=highest
    )
    imag_out = jnp.einsum("ut,bckt->bcku", real_table, imag_in, precision=highest) + jnp.einsum(
        "ut,bckt->bcku", imag_table, real_in, precision=highest
    )
    power = jnp.mean(real_out * real_out + imag_out * imag_out, axis=2)
    return jnp.transpose(power, (1, 2, 0))


def combine(beam_weights, feed_data):
    product = jnp.einsum(
        "cpbi,cqsi->bcpqs", beam_weights, feed_data, preferred_element_type=jnp.float32
    )
    real_part = product[:, :, 0, 0] - product[:, :, 1, 1]
    imag_part = product[:, :, 0, 1] + product[:, :, 1, 0]
    return jnp.stack([real_part, imag_part], axis=2)


def on_device(voltages, weights, input_map, beam_order):
    local_chan = weights.shape[0]
    spectra = SPECTRA
    spectrum = channelize(voltages, CHAN, BAND_LO, WIN, TAPS, spectra)
    turned = lax.all_to_all(spectrum, "dev", split_axis=0, concat_axis=2, tiled=True)
    group_in = turned.shape[2]
    inverse = (
        jnp.zeros((group_in,), jnp.int32).at[input_map].set(jnp.arange(group_in, dtype=jnp.int32))
    )
    local_data = jnp.take(turned.reshape(local_chan, 2, spectra, group_in), inverse, axis=3)
    ordered = jnp.take(weights, beam_order, axis=2)
    owned = lax.psum_scatter(combine(ordered, local_data), "grp", scatter_dimension=0, tiled=True)
    return detect(owned, UPCH)


def solution(mesh):
    placed = (P(("grp", "dev"), None), P("dev", None, None, "grp"), P("grp"), P())
    return jax.shard_map(
        on_device, mesh=mesh, in_specs=placed, out_specs=P("dev", None, "grp"), check_vma=False
    )
```

profile of v0, /device:TPU:2, one launch (start us, length us, event | category | flops | bytes accessed | tf_op | source)
XLA Modules:
  0.0 327.3 jit_solution(5433925140470516375)
XLA Ops:
  6.5 0.2 fusion.32
  6.7 15.3 %fusion.98 = (f32[8,128,2048]{2,0,1:T(8,128)}, f32[8,128,2048]{2,0,1:T(8,128)}, f32[8,128,2048]{2,0,1:T(8,128)}, f32[8,128,2048]{2,0,1:T(8,128)}) fusion(bf16[8,131,2048]{2,0,1:T(8,128)(2,1)} %bitcast.61), kind=kLoop, calls=%fused_computation.137 | loop fusion | bytes 67108864 | tf_op jit(solution)/shard_map/slice | solution.py:38
  22.1 18.2 %multiply_convert_fusion.1 = (bf16[512,1,2048]{2,0,1:T(8,128)(2,1)S(1)}, bf16[512,1,2048]{2,0,1:T(8,128)(2,1)S(1)}) fusion(s32[512]{0:T(512)S(1)} %iota_add_fusion.2), kind=kLoop, calls=%fused_computation.31 | loop fusion | flops 19922944 | bytes 4196352 | tf_op jit(solution)/shard_map/convert.1
  40.2 0.4 pad_maximum_fusion.1
  40.6 6.3 %copy.49 = bf16[512,2,2048]{2,1,0:T(2,128)(2,1)} copy(bf16[512,2,2048]{2,0,1:T(8,128)(2,1)S(1)} %pad_maximum_fusion.1) | data formatting | bytes 8388608 | tf_op jit(solution)/shard_map/stack | solution.py:30
  46.9 7.2 %reshape.213 = bf16[1024,2048,1]{1,0,2:T(8,128)(2,1)} reshape(bf16[512,2,2048]{2,1,0:T(2,128)(2,1)} %copy.49) | data formatting | bytes 8388608 | tf_op jit(solution)/shard_map/convert_element_type | solution.py:31
  54.1 54.9 %convert_bitcast_fusion = bf16[1024,128,8]{0,1,2:T(8,128)(2,1)S(1)} fusion(bf16[1024,2048,1]{1,0,2:T(8,128)(2,1)} %reshape.213, f32[8,128,2048]{2,0,1:T(8,128)} %get-tuple-element.8, f32[8,128,2048]{2,0,1:T(8,128)} %get-tuple-element.7, f32[8,128,2048]{2,0,1:T(8,128)} %get-tuple-element.6, f32[8,128,2048]{2,0,1:T(8,128)} %get-tuple-element.5, ...), kind=kOutput, calls=%fused_computation.38 | convolution fusion | flops 4312793088 | bytes 39878656 | tf_op jit(solution)/shard_map/kn,isn->ksi/dot_general | solution.py:42
  109.0 0.0 copy-start
  109.0 2.9 copy.50
  111.9 14.2 %all-to-all-start = ((bf16[1024,128,8]{1,2,0:T(8,128)(2,1)}), bf16[1024,128,8]{1,2,0:T(8,128)(2,1)S(1)}, u32[]{:S(2)}, u32[]{:S(2)}) async-start(bf16[1024,128,8]{1,2,0:T(8,128)(2,1)} %copy.50), calls=%async_computation | async-start | bytes 4194304 | tf_op jit(solution)/shard_map/all_to_all | solution.py:84
  126.2 0.0 reduce-scatter.2.cloned.1.call-start
  126.2 0.0 copy-done
  126.3 0.0 copy-start.1
  126.3 35.0 %gather_fusion.1 = bf16[512,16,2,256]{3,0,2,1:T(8,128)(2,1)} fusion(bf16[16,2,512,256]{3,2,1,0:T(8,128)(2,1)} %param.5, s32[1024]{0:T(1024)S(1)} %pad_clamp_fusion), kind=kCustom, calls=%fused_computation.1 | custom fusion | bytes 16779264 | tf_op jit(solution)/shard_map/jit(_take)/gather | solution.py:90
  161.3 0.0 copy-done.1
  161.3 1.4 scatter_custom_fusion
  162.8 16.4 %all-to-all-done = bf16[1024,128,8]{1,2,0:T(8,128)(2,1)S(1)} async-done(((bf16[1024,128,8]{1,2,0:T(8,128)(2,1)}), bf16[1024,128,8]{1,2,0:T(8,128)(2,1)S(1)}, u32[]{:S(2)}, u32[]{:S(2)}) %all-to-all-start) | async-done | bytes 2097184 | tf_op jit(solution)/shard_map/all_to_all | solution.py:84
  179.2 0.6 copy.51
  179.8 2.7 copy.52
  182.5 2.7 gather_fusion
  185.1 0.9 select_bitcast_fusion
  186.1 13.2 %convolution_bitcast_fusion = f32[512,16,2,2,128]{0,4,2,3,1:T(8,128)} fusion(bf16[512,16,2,256]{3,0,2,1:T(8,128)(2,1)} %gather_fusion.1, pred[512]{0:T(512)(128)(4,1)S(1)} %compare_and_fusion, bf16[16,2,128,256,1]{2,0,1,3,4:T(8,128)(2,1)S(1)} %select_bitcast_fusion), kind=kOutput, calls=%fused_computation.3 | convolution fusion | flops 2151677952 | bytes 27263488 | tf_op jit(solution)/shard_map/cpbi,cqsi->bcpqs/dot_general | solution.py:72
  199.2 4.5 %fusion.10 = f32[512,16,1,128]{0,3,1,2:T(8,128)S(1)} fusion(f32[512,16,2,2,128]{0,4,2,3,1:T(8,128)} %convolution_bitcast_fusion), kind=kLoop, calls=%fused_computation.23 | loop fusion | flops 1048576 | bytes 12582912 | tf_op jit(solution)/shard_map/add | solution.py:76
  203.7 4.5 %fusion.12 = f32[512,16,1,128]{0,3,1,2:T(8,128)S(1)} fusion(f32[512,16,2,2,128]{0,4,2,3,1:T(8,128)} %convolution_bitcast_fusion), kind=kLoop, calls=%fused_computation.26 | loop fusion | flops 1048576 | bytes 12582912 | tf_op jit(solution)/shard_map/sub | solution.py:75
  208.2 4.2 %pad_maximum_fusion = f32[512,16,2,128]{0,3,1,2:T(8,128)} fusion(f32[512,16,1,128]{0,3,1,2:T(8,128)S(1)} %fusion.10, f32[512,16,1,128]{0,3,1,2:T(8,128)S(1)} %fusion.12), kind=kLoop, calls=%fused_computation.4 | loop fusion | flops 2097152 | bytes 16777216 | tf_op jit(solution)/shard_map/stack | solution.py:77
  212.5 10.5 %copy.56 = f32[512,16,2,128]{3,1,2,0:T(8,128)} copy(f32[512,16,2,128]{0,3,1,2:T(8,128)} %pad_maximum_fusion) | data formatting | bytes 16777216 | tf_op jit(solution)/shard_map/stack | solution.py:77
  223.0 0.0 reduce-scatter.2.cloned.1.call-update
  223.0 90.2 %reduce-scatter.2.cloned.1.call-done = f32[64,16,2,128]{3,1,2,0:T(8,128)} async-done(((f32[512,16,2,128]{3,1,2,0:T(8,128)}), f32[64,16,2,128]{3,1,2,0:T(8,128)}) %reduce-scatter.2.cloned.1.call-update) | async-done | bytes 1048592 | tf_op jit(solution)/shard_map/reduce_scatter | solution.py:91
  313.2 1.8 copy.57
  315.0 1.1 fusion.26
  316.1 1.1 fusion.27
  317.1 1.1 fusion.24
  318.2 1.1 fusion.25
  319.4 0.7 multiply_bitcast_fusion
  (10 shorter events, 0.0 us)
Async XLA Ops:
  109.0 17.2 %copy-start = (s32[512]{0:T(512)S(1)}, s32[512]{0:T(512)}, u32[]{:S(2)}) copy-start(s32[512]{0:T(512)} %param.7) | copy-start | bytes 6148
  111.9 67.2 %all-to-all-start = ((bf16[1024,128,8]{1,2,0:T(8,128)(2,1)}), bf16[1024,128,8]{1,2,0:T(8,128)(2,1)S(1)}, u32[]{:S(2)}, u32[]{:S(2)}) async-start(bf16[1024,128,8]{1,2,0:T(8,128)(2,1)} %copy.50), calls=%async_computation | async-start | bytes 4194304 | tf_op jit(solution)/shard_map/all_to_all | solution.py:84
  126.2 187.0 %reduce-scatter.2.cloned.1.call-start = ((), (), s32[]{:S(2)}) async-start(), calls=%async_computation.2 | async-start | bytes 9437184 | tf_op jit(solution)/shard_map/reduce_scatter | solution.py:91
  126.3 35.0 %copy-start.1 = (s32[256]{0:T(256)S(1)}, s32[256]{0:T(256)}, u32[]{:S(2)}) copy-start(s32[256]{0:T(256)} %param.6) | copy-start | bytes 3076
Sparse Core Ops, SparseCore 0:
  223.1 89.9 reduce-scatter.1
where the time goes:
time: 334 us; the launch traced here: 327 us
  waiting for transfers between devices  107 us (32%)
  local copies, waits for them, and re-layouts  86.4 us (26%)
  matrix products  72.4 us (22%)
  other arithmetic  33.6 us (10%)
  starting transfers between devices  14.3 us (4%)
  between operations  14.1 us (4%)
    reduce_scatter x1, waiting for transfers between devices, on_device(): lax.psum_scatter(combine(ordered, local_data), 'grp', scatter_dimension=0...  90.2 us
    dot_general x1, matrix products, channelize(): jnp.einsum('kn,isn->ksi', transform_table(chan, first, count), summed, pr...  54.9 us
    gather x1, local copies, waits for them, and re-layouts, on_device(): ordered = jnp.take(weights, beam_order, axis=2)  35 us
    another operation x1, other arithmetic  18.2 us
    all_to_all x1, waiting for transfers between devices, on_device(): lax.all_to_all(spectrum, 'dev', split_axis=0, concat_axis=2, tiled=True)  16.4 us
    slice x2, local copies, waits for them, and re-layouts, channelize(): summed = taper[0] * frames[:, 0:spectra, :]  15.3 us
    all_to_all x1, starting transfers between devices, on_device(): lax.all_to_all(spectrum, 'dev', split_axis=0, concat_axis=2, tiled=True)  14.2 us
    dot_general x1, matrix products, combine(): jnp.einsum('cpbi,cqsi->bcpqs', beam_weights, feed_data, preferred_element...  13.2 us
  transfers between devices with their start and end apart: 2, of which 2 were waited for; matrix products, arithmetic and copies ran while one was open for 11% of the time, Pallas kernels for 0%

commit v1 on v0

v1 whole, which is shorter than its diff:
```python
import math

import jax
import jax.numpy as jnp
import numpy as np
from jax import lax
from jax.experimental import pallas as pl
from jax.experimental.pallas import tpu as pltpu
from jax.sharding import Mesh
from jax.sharding import PartitionSpec as P

CHAN = 1024
NFFT = 2048
TAPS = 4
UPCH = 16
WIN = 512
SPECTRA = 128
BAND_LO = 256
LANES = 128
OWN = 8
NT = NFFT // LANES
MIB = 1 << 20


def taper_table():
    index = np.arange(TAPS * NFFT, dtype=np.float64)
    centred = (index - TAPS * NFFT / 2.0 + 0.5) / NFFT
    window = 0.5 - 0.5 * np.cos(2.0 * math.pi * (index + 0.5) / (TAPS * NFFT))
    return (np.sinc(centred) * window).astype(np.float32).reshape(TAPS, NFFT)


def transform_table():
    chan_ids = BAND_LO + np.arange(WIN)
    angles = 2.0 * math.pi * ((chan_ids[:, None] * np.arange(NFFT)[None, :]) % NFFT) / NFFT
    stacked = np.stack([np.cos(angles), -np.sin(angles)], axis=1) / math.sqrt(CHAN)
    return stacked.reshape(2 * WIN, NFFT).astype(jnp.bfloat16)


def channelize_kernel(volts_ref, taper_ref, table_ref, out_ref, fir_ref, frames_ref, turn_ref):
    def fir_tile(nt, _):
        lane = pl.multiple_of(nt * LANES, LANES)
        taps = [taper_ref[t, :, pl.ds(lane, LANES)] for t in range(TAPS)]

        def load(frame):
            at = pl.multiple_of(frame * NFFT + lane, LANES)
            return volts_ref[:, pl.ds(at, LANES)].astype(jnp.float32)

        def spectra(s0, held):
            held = list(held)
            for k in range(16):
                s = s0 * 16 + k
                held.append(load(s + TAPS - 1))
                total = taps[0] * held[0]
                for t in range(1, TAPS):
                    total = total + taps[t] * held[t]
                held = held[1:]
                fir_ref[pl.ds(pl.multiple_of(s * OWN, OWN), OWN), :] = total
            return tuple(held)

        lax.fori_loop(0, SPECTRA // 16, spectra, tuple(load(t) for t in range(TAPS - 1)))
        for i in range(OWN):
            frames_ref[pl.ds(i * SPECTRA, SPECTRA), pl.ds(lane, LANES)] = fir_ref[
                pl.ds(i, SPECTRA, stride=OWN), :
            ].astype(jnp.bfloat16)
        return 0

    lax.fori_loop(0, NT, fir_tile, 0)
    rows = 256

    def transform(block, _):
        at = pl.multiple_of(block * rows, rows)
        table = table_ref[pl.ds(at, rows), :]
        for pair in range(OWN // 2):
            part = lax.dot_general(
                table,
                frames_ref[pl.ds(pair * 2 * SPECTRA, 2 * SPECTRA), :],
                (((1,), (1,)), ((), ())),
                preferred_element_type=jnp.float32,
            )
            for half in range(2):
                turn_ref[pl.ds(pair * 2 + half, rows, stride=OWN), :] = part[
                    :, half * SPECTRA : (half + 1) * SPECTRA
                ]
        out_ref[pl.ds(pl.multiple_of(at * OWN, rows * OWN), rows * OWN), :] = turn_ref[...].astype(jnp.bfloat16)
        return 0

    lax.fori_loop(0, 2 * WIN // rows, transform, 0)


def channelize(volts):
    taper = jnp.asarray(np.broadcast_to(taper_table()[:, None, :], (TAPS, OWN, NFFT)).copy())
    table = jnp.asarray(transform_table())
    return pl.pallas_call(
        channelize_kernel,
        out_shape=jax.ShapeDtypeStruct((2 * WIN * OWN, SPECTRA), jnp.bfloat16),
        scratch_shapes=[
            pltpu.VMEM((SPECTRA * OWN, LANES), jnp.float32),
            pltpu.VMEM((SPECTRA * OWN, NFFT), jnp.bfloat16),
            pltpu.VMEM((256 * OWN, SPECTRA), jnp.float32),
        ],
        compiler_params=pltpu.CompilerParams(vmem_limit_bytes=48 * MIB),
    )(volts, taper, table)


def weight_kernel(order_ref, map_ref, weights_ref, out_ref, pick_ref, place_ref):
    beams = weights_ref.shape[2]
    feeds = weights_ref.shape[3]

    @pl.when(pl.program_id(0) == 0)
    def _():
        ids = lax.broadcasted_iota(jnp.int32, (beams, beams), 1)
        pick_ref[...] = jnp.where(order_ref[...] == ids, 1.0, 0.0).astype(jnp.bfloat16)
        feed = lax.broadcasted_iota(jnp.int32, (feeds, 2 * feeds), 0)
        part = (lax.broadcasted_iota(jnp.int32, (feeds, 2 * feeds), 1) // OWN) % 2
        match = jnp.where(map_ref[...] == feed, 1.0, 0.0)
        of_real = jnp.where(part == 0, match, 0.0).astype(jnp.bfloat16)
        of_imag = jnp.where(part == 1, match, 0.0).astype(jnp.bfloat16)
        place_ref[0:feeds, 0 : 2 * feeds] = of_real
        place_ref[feeds:, 0 : 2 * feeds] = -of_imag
        place_ref[0:feeds, 2 * feeds :] = of_imag
        place_ref[feeds:, 2 * feeds :] = of_real

    wide = jnp.concatenate([weights_ref[0, 0], weights_ref[0, 1]], axis=1)
    picked = jnp.dot(pick_ref[...], wide, preferred_element_type=jnp.float32).astype(jnp.bfloat16)
    out_ref[0] = jnp.dot(picked, place_ref[...], preferred_element_type=jnp.float32).astype(jnp.bfloat16)


def arrange_weights(weights, order, inputs_map):
    chans, _, beams, feeds = weights.shape
    spread = jnp.broadcast_to(inputs_map.reshape(-1, 1, OWN), (feeds // OWN, 2, OWN)).reshape(1, 2 * feeds)
    return pl.pallas_call(
        weight_kernel,
        grid=(chans,),
        out_shape=jax.ShapeDtypeStruct((chans, beams, 4 * feeds), jnp.bfloat16),
        in_specs=[
            pl.BlockSpec((beams, 1), lambda c: (0, 0)),
            pl.BlockSpec((1, 2 * feeds), lambda c: (0, 0)),
            pl.BlockSpec((1, 2, beams, feeds), lambda c: (c, 0, 0, 0)),
        ],
        out_specs=pl.BlockSpec((1, beams, 4 * feeds), lambda c: (c, 0, 0)),
        scratch_shapes=[
            pltpu.VMEM((beams, beams), jnp.bfloat16),
            pltpu.VMEM((2 * feeds, 4 * feeds), jnp.bfloat16),
        ],
        compiler_params=pltpu.CompilerParams(vmem_limit_bytes=32 * MIB),
        cost_estimate=pl.CostEstimate(
            flops=2 * chans * beams * 2 * feeds * (beams + 4 * feeds),
            bytes_accessed=3 * 2 * weights.size,
            transcendentals=0,
        ),
    )(order.reshape(beams, 1), spread, weights)


def combine_kernel(weights_ref, data_ref, keep_ref, send_ref):
    beams, wide = weights_ref.shape[1:]
    spectra = data_ref.shape[3]
    half = beams // 2
    data = data_ref[:, 0].reshape(wide // 2, spectra)
    for part in range(2):
        product = jnp.dot(
            weights_ref[0, :, part * (wide // 2) : (part + 1) * (wide // 2)],
            data,
            preferred_element_type=jnp.float32,
        )
        keep_ref[:, 0, part] = product[:half].reshape(4, half // 4, spectra)
        send_ref[:, 0, part] = product[half:].reshape(4, half // 4, spectra).astype(jnp.bfloat16)


def combine(arranged, data):
    chans, beams, wide = arranged.shape
    sources, _, rows, spectra = data.shape
    shape = (4, chans, 2, beams // 8, spectra)
    block = pl.BlockSpec((4, 1, 2, beams // 8, spectra), lambda c: (0, c, 0, 0, 0))
    return pl.pallas_call(
        combine_kernel,
        grid=(chans,),
        out_shape=(jax.ShapeDtypeStruct(shape, jnp.float32), jax.ShapeDtypeStruct(shape, jnp.bfloat16)),
        in_specs=[
            pl.BlockSpec((1, beams, wide), lambda c: (c, 0, 0)),
            pl.BlockSpec((sources, 1, rows, spectra), lambda c: (0, c, 0, 0)),
        ],
        out_specs=(block, block),
        compiler_params=pltpu.CompilerParams(vmem_limit_bytes=32 * MIB),
    )(arranged, data)


def fine_tables():
    steps = np.arange(UPCH)
    angles = 2.0 * math.pi * (np.outer(steps, steps) % UPCH) / UPCH
    eye = np.eye(SPECTRA // UPCH)
    real = np.kron(eye, np.cos(angles) / math.sqrt(UPCH))
    imag = np.kron(eye, -np.sin(angles) / math.sqrt(UPCH))
    turn = np.block([[real, imag], [-imag, real]]).astype(np.float32)
    mean = np.tile(np.eye(UPCH) * UPCH / SPECTRA, (1, SPECTRA // UPCH)).astype(np.float32)
    return turn, mean


def detect_kernel(keep_ref, come_ref, turn_ref, mean_ref, out_ref):
    chans, _, beams, spectra = keep_ref.shape
    total = keep_ref[...] + come_ref[...].astype(jnp.float32)
    both = jnp.concatenate(
        [total[:, 0].reshape(chans * beams, spectra), total[:, 1].reshape(chans * beams, spectra)], axis=1
    )
    sub = jnp.dot(both, turn_ref[...], preferred_element_type=jnp.float32, precision=lax.Precision.HIGHEST)
    power = sub[:, :spectra] * sub[:, :spectra] + sub[:, spectra:] * sub[:, spectra:]
    mean = lax.dot_general(
        mean_ref[...],
        power,
        (((1,), (1,)), ((), ())),
        preferred_element_type=jnp.float32,
        precision=lax.Precision.HIGHEST,
    )
    for chan in range(chans):
        out_ref[chan] = mean[:, chan * beams : (chan + 1) * beams]


def detect(keep, come):
    chans, _, beams, _ = keep.shape
    turn, mean = fine_tables()
    return pl.pallas_call(
        detect_kernel,
        out_shape=jax.ShapeDtypeStruct((chans, UPCH, beams), jnp.float32),
        compiler_params=pltpu.CompilerParams(vmem_limit_bytes=32 * MIB),
    )(keep, come, jnp.asarray(turn), jnp.asarray(mean))


def swap(value, axis, distance, size):
    return lax.ppermute(value, axis, [(k, k ^ distance) for k in range(size)])


def on_device(voltages, weights, input_map, beam_order):
    chans = weights.shape[0]
    spectrum = channelize(voltages)
    devices = 2 * WIN // (2 * chans)
    turned = lax.all_to_all(
        spectrum.reshape(devices, chans * 2 * OWN, SPECTRA), ("y", "zh", "x"), split_axis=0, concat_axis=0, tiled=True
    )
    core, z = lax.axis_index("core"), lax.axis_index("zl")
    blocks = beam_order.reshape(4, 2, -1)
    near = jnp.where(core == 0, blocks, blocks[:, ::-1])
    near = jnp.where(z % 2 == 0, near, near.reshape(2, 2, 2, -1)[:, ::-1].reshape(near.shape))
    near = jnp.where(z // 2 == 0, near, near.reshape(2, 2, 2, -1)[::-1].reshape(near.shape))
    order = jnp.transpose(near, (1, 0, 2)).reshape(-1)
    arranged = arrange_weights(weights, order, input_map)
    keep, send = combine(arranged, turned.reshape(devices, chans, 2 * OWN, SPECTRA))
    total = keep + swap(send, "core", 1, 2).astype(jnp.float32)
    total = total.reshape((2, 2) + total.shape[1:])
    half = chans // 2
    first, second = total[:, :, :half], total[:, :, half:]
    first_in = swap(first[:, 1].astype(jnp.bfloat16), "zl", 1, 4)
    second_in = swap(second[1].astype(jnp.bfloat16), "zl", 2, 4)
    first = first[:, 0] + first_in.astype(jnp.float32)
    second = second[0] + second_in.astype(jnp.float32)
    first_in = swap(first[1].astype(jnp.bfloat16), "zl", 2, 4)
    second_in = swap(second[1].astype(jnp.bfloat16), "zl", 1, 4)
    return jnp.concatenate([detect(first[0], first_in), detect(second[0], second_in)], axis=0)


def solution(mesh):
    fine = Mesh(mesh.devices.reshape(4, 2, 4, 2, 4), ("zl", "core", "y", "zh", "x"))
    grp, dev = ("zl", "core"), ("y", "zh", "x")
    placed = (P(grp + dev, None), P(dev, None, None, grp), P(grp), P())
    return jax.shard_map(on_device, mesh=fine, in_specs=placed, out_specs=P(dev, None, grp), check_vma=False)
```

time: 334 us -> 149 us (0.45); the launches traced: 327 us -> 149 us
  local copies, waits for them, and re-layouts: 86.4 us -> 6.43 us
  matrix products: 72.4 us -> 0 us
  Pallas kernels: 0 us -> 48.6 us
  waiting for transfers between devices: 107 us -> 70.8 us
  other arithmetic: 33.6 us -> 2.81 us
  between operations: 14.1 us -> 0.24 us
  starting transfers between devices: 14.3 us -> 19.8 us
    reduce_scatter x1 -> x0, waiting for transfers between devices: 90.2 us -> none  [on_device(): lax.psum_scatter(combine(ordered, local_data), 'grp', scatter_dimension=0...]
    dot_general x6 -> x0, matrix products: 72.4 us -> none  [the longest x1 54.9 us: channelize(): jnp.einsum('kn,isn->ksi', transform_table(chan, first, count), summed, pr...]
    pallas_call x0 -> x5, Pallas kernels: none -> 48.6 us  [the longest x1 17.4 us: arrange_weights(): pl.pallas_call(weight_kernel, grid=(chans,), out_shape=jax.ShapeDtypeStru...]
    ppermute x0 -> x5, waiting for transfers between devices: none -> 39.3 us  [swap(): return lax.ppermute(value, axis, [(k, k ^ distance) for k in range(size)])]
    gather x2 -> x0, local copies, waits for them, and re-layouts: 37.6 us -> none  [the longest x1 35 us: on_device(): ordered = jnp.take(weights, beam_order, axis=2)]
    another operation x3 -> x1, other arithmetic: 22.8 us -> 0.54 us
    another operation x2 -> x1, local copies, waits for them, and re-layouts: 16.8 us -> 0.2 us  [arrange_weights(): order.reshape(beams, 1)]
    slice x2 -> x0, local copies, waits for them, and re-layouts: 15.3 us -> none  [channelize(): summed = taper[0] * frames[:, 0:spectra, :]]
  transfers between devices with their start and end apart: 2 -> 6, of which waited for: 2 -> 6; matrix products, arithmetic and copies ran while one was open for 11% -> 0% of each run, Pallas kernels for 0% -> 13%
where the time goes in v1:
time: 149 us
  waiting for transfers between devices  70.8 us (48%)
  Pallas kernels  48.6 us (33%)
  starting transfers between devices  19.8 us (13%)
  local copies, waits for them, and re-layouts  6.43 us (4%)
  other arithmetic  2.81 us (2%)
    ppermute x5, waiting for transfers between devices, swap(): return lax.ppermute(value, axis, [(k, k ^ distance) for k in range(size)])  39.3 us
    all_to_all x1, waiting for transfers between devices, on_device(): lax.all_to_all(spectrum.reshape(devices, chans * 2 * OWN, SPECTRA), ('y',...  31.5 us
    pallas_call x1, Pallas kernels, arrange_weights(): pl.pallas_call(weight_kernel, grid=(chans,), out_shape=jax.ShapeDtypeStru...  17.4 us
    pallas_call x1, Pallas kernels, combine(): pl.pallas_call(combine_kernel, grid=(chans,), out_shape=(jax.ShapeDtypeSt...  14.5 us
    all_to_all x1, starting transfers between devices, on_device(): lax.all_to_all(spectrum.reshape(devices, chans * 2 * OWN, SPECTRA), ('y',...  14.4 us
    pallas_call x1, Pallas kernels, channelize(): pl.pallas_call(channelize_kernel, out_shape=jax.ShapeDtypeStruct((2 * WIN...  14.2 us
    unnamed x14, local copies, waits for them, and re-layouts  5.67 us
    ppermute x5, starting transfers between devices, swap(): return lax.ppermute(value, axis, [(k, k ^ distance) for k in range(size)])  5.45 us
  transfers between devices with their start and end apart: 6, of which 6 were waited for; matrix products, arithmetic and copies ran while one was open for 0% of the time, Pallas kernels for 13%

profile of v1, /device:TPU:2, one launch (start us, length us, event | category | flops | bytes accessed | tf_op | source)
XLA Modules:
  0.0 148.7 jit_solution(13981696512320468949)
XLA Ops:
  0.0 0.0 copy-start.2
  0.0 0.9 copy-done.2
  1.0 14.2 %shard_map.101 = bf16[8192,128]{1,0:T(8,128)(2,1)S(1)} custom-call(bf16[8,268288]{1,0:T(8,128)(2,1)} %volts_ref.1, f32[4,8,2048]{2,1,0:T(8,128)S(1)} %copy-done.2, bf16[1024,2048]{1,0:T(8,128)(2,1)} %constant.46.clone.table_ref), custom_call_target="tpu_custom_call" | custom-call | tf_op jit(solution)/shard_map/pallas_call | solution.py:93
  15.2 0.0 copy-start
  15.2 1.3 copy-done
  16.5 0.0 copy-start.5
  16.5 0.0 copy-start.6
  16.5 14.4 %all-to-all-start = ((bf16[32,256,128]{2,1,0:T(8,128)(2,1)}), bf16[32,256,128]{2,1,0:T(8,128)(2,1)S(1)}, u32[]{:S(2)}, u32[]{:S(2)}) async-start(bf16[32,256,128]{2,1,0:T(8,128)(2,1)} %bitcast.36), calls=%async_computation | async-start | bytes 4194304 | tf_op jit(solution)/shard_map/all_to_all | solution.py:235
  30.9 0.0 copy-done.5
  30.9 0.1 reshape.33
  31.1 0.0 copy-done.6
  31.1 0.1 broadcast_in_dim.7
  31.2 0.1 reshape.38.map_ref
  31.3 0.2 reshape_reshape.4.order_ref
  31.6 0.0 copy-start.4
  31.6 3.4 %copy-done.4 = bf16[16,2,512,256]{3,2,1,0:T(8,128)(2,1)S(1)} copy-done((bf16[16,2,512,256]{3,2,1,0:T(8,128)(2,1)S(1)}, bf16[16,2,512,256]{3,2,1,0:T(8,128)(2,1)}, u32[]{:S(2)}) %copy-start.4) | copy-done | bytes 8388632
  34.9 17.4 %shard_map.100.weights_ref = bf16[16,512,1024]{2,1,0:T(8,128)(2,1)} custom-call(s32[512,1]{1,0:T(8,128)S(1)} %reshape_reshape.4.order_ref, s32[1,512]{1,0:T(1,128)S(1)} %reshape.38.map_ref, bf16[16,2,512,256]{3,2,1,0:T(8,128)(2,1)S(1)} %copy-done.4), custom_call_target="tpu_custom_call" | custom-call | flops 12884901888 | bytes 25165824 | tf_op jit(solution)/shard_map/pallas_call | solution.py:131
  52.4 31.5 %all-to-all-done = bf16[32,256,128]{2,1,0:T(8,128)(2,1)S(1)} async-done(((bf16[32,256,128]{2,1,0:T(8,128)(2,1)}), bf16[32,256,128]{2,1,0:T(8,128)(2,1)S(1)}, u32[]{:S(2)}, u32[]{:S(2)}) %all-to-all-start) | async-done | bytes 2097184 | tf_op jit(solution)/shard_map/all_to_all | solution.py:235
  83.9 14.5 %shard_map.102 = (f32[4,16,2,64,128]{4,3,2,1,0:T(8,128)S(1)}, bf16[4,16,2,64,128]{4,3,2,1,0:T(8,128)(2,1)S(1)}) custom-call(bf16[16,512,1024]{2,1,0:T(8,128)(2,1)} %shard_map.100.weights_ref, bf16[32,16,16,128]{3,2,1,0:T(8,128)(2,1)S(1)} %bitcast.35), custom_call_target="tpu_custom_call" | custom-call | tf_op jit(solution)/shard_map/pallas_call | solution.py:174
  98.4 0.1 collective-permute-start
  98.5 4.1 %collective-permute-done = bf16[4,16,2,64,128]{4,3,2,1,0:T(8,128)(2,1)S(1)} collective-permute-done((bf16[4,16,2,64,128]{4,3,2,1,0:T(8,128)(2,1)S(1)}, bf16[4,16,2,64,128]{4,3,2,1,0:T(8,128)(2,1)S(1)}, u32[]{:S(2)}, u32[]{:S(2)}) %collective-permute-start) | collective-permute-done | bytes 2097184 | tf_op jit(solution)/shard_map/ppermute | solution.py:228
  102.6 1.1 convert_add_fusion
  103.7 0.5 convert.10
  104.4 0.0 copy-start.1
  104.4 0.0 copy-start.3
  104.4 2.2 %collective-permute-start.1 = (bf16[2,8,2,64,128]{4,3,2,1,0:T(8,128)(2,1)S(1)}, bf16[2,8,2,64,128]{4,3,2,1,0:T(8,128)(2,1)S(1)}, u32[]{:S(2)}, u32[]{:S(2)}) collective-permute-start(bf16[2,8,2,64,128]{4,3,2,1,0:T(8,128)(2,1)S(1)} %slice_bitcast_fusion.5), channel_id=1, source_target_pairs={{0,64},{64,0},{128,192},{192,128},{1,65},{65,1},{129,193},{193,129... | collective-permute-start | bytes 1572872 | tf_op jit(solution)/shard_map/ppermute | solution.py:228
  106.6 0.6 collective-permute-start.3
  107.2 22.2 %collective-permute-done.1 = bf16[2,8,2,64,128]{4,3,2,1,0:T(8,128)(2,1)S(1)} collective-permute-done((bf16[2,8,2,64,128]{4,3,2,1,0:T(8,128)(2,1)S(1)}, bf16[2,8,2,64,128]{4,3,2,1,0:T(8,128)(2,1)S(1)}, u32[]{:S(2)}, u32[]{:S(2)}) %collective-permute-start.1) | collective-permute-done | bytes 524320 | tf_op jit(solution)/shard_map/ppermute | solution.py:228
  129.4 3.1 %collective-permute-done.3 = bf16[2,8,2,64,128]{4,3,2,1,0:T(8,128)(2,1)S(1)} collective-permute-done((bf16[2,8,2,64,128]{4,3,2,1,0:T(8,128)(2,1)S(1)}, bf16[2,8,2,64,128]{4,3,2,1,0:T(8,128)(2,1)S(1)}, u32[]{:S(2)}, u32[]{:S(2)}) %collective-permute-start.3) | collective-permute-done | bytes 524320 | tf_op jit(solution)/shard_map/ppermute | solution.py:228
  132.5 0.5 fusion.1
  133.0 0.1 collective-permute-start.4
  133.2 2.5 %collective-permute-start.2 = (bf16[8,2,64,128]{3,2,1,0:T(8,128)(2,1)S(1)}, bf16[8,2,64,128]{3,2,1,0:T(8,128)(2,1)S(1)}, u32[]{:S(2)}, u32[]{:S(2)}) collective-permute-start(bf16[8,2,64,128]{3,2,1,0:T(8,128)(2,1)S(1)} %fusion.2), channel_id=1, source_target_pairs={{0,128},{64,192},{128,0},{192,64},{1,129},{65,193},{129,1},{193,65... | collective-permute-start | bytes 786440 | tf_op jit(solution)/shard_map/ppermute | solution.py:228
  135.6 0.1 slice_bitcast_fusion.2
  135.7 8.0 %collective-permute-done.4.come_ref = bf16[8,2,64,128]{3,2,1,0:T(8,128)(2,1)S(1)} collective-permute-done((bf16[8,2,64,128]{3,2,1,0:T(8,128)(2,1)S(1)}, bf16[8,2,64,128]{3,2,1,0:T(8,128)(2,1)S(1)}, u32[]{:S(2)}, u32[]{:S(2)}) %collective-permute-start.4) | collective-permute-done | bytes 262176 | tf_op jit(solution)/shard_map/ppermute | solution.py:228
  143.7 0.0 copy-done.1
  143.7 0.0 copy-done.3
  143.7 1.2 shard_map.104
  144.9 1.9 %collective-permute-done.2.come_ref = bf16[8,2,64,128]{3,2,1,0:T(8,128)(2,1)S(1)} collective-permute-done((bf16[8,2,64,128]{3,2,1,0:T(8,128)(2,1)S(1)}, bf16[8,2,64,128]{3,2,1,0:T(8,128)(2,1)S(1)}, u32[]{:S(2)}, u32[]{:S(2)}) %collective-permute-start.2) | collective-permute-done | bytes 262176 | tf_op jit(solution)/shard_map/ppermute | solution.py:228
  146.8 1.2 shard_map.103
  148.0 0.7 pad_maximum_fusion
  (12 shorter events, 0.2 us)
Async XLA Ops:
  0.0 0.9 copy-start.2
  15.2 1.3 copy-start
  16.5 14.4 %copy-start.5 = (s32[512]{0:T(512)S(1)}, s32[512]{0:T(512)}, u32[]{:S(2)}) copy-start(s32[512]{0:T(512)} %param.13) | copy-start | bytes 6148
  16.5 14.6 %copy-start.6 = (s32[256]{0:T(256)S(1)}, s32[256]{0:T(256)}, u32[]{:S(2)}) copy-start(s32[256]{0:T(256)} %param.12) | copy-start | bytes 3076
  16.5 67.4 %all-to-all-start = ((bf16[32,256,128]{2,1,0:T(8,128)(2,1)}), bf16[32,256,128]{2,1,0:T(8,128)(2,1)S(1)}, u32[]{:S(2)}, u32[]{:S(2)}) async-start(bf16[32,256,128]{2,1,0:T(8,128)(2,1)} %bitcast.36), calls=%async_computation | async-start | bytes 4194304 | tf_op jit(solution)/shard_map/all_to_all | solution.py:235
  31.6 3.4 %copy-start.4 = (bf16[16,2,512,256]{3,2,1,0:T(8,128)(2,1)S(1)}, bf16[16,2,512,256]{3,2,1,0:T(8,128)(2,1)}, u32[]{:S(2)}) copy-start(bf16[16,2,512,256]{3,2,1,0:T(8,128)(2,1)} %weights_ref.1) | copy-start | bytes 25165828
  98.4 4.2 %collective-permute-start = (bf16[4,16,2,64,128]{4,3,2,1,0:T(8,128)(2,1)S(1)}, bf16[4,16,2,64,128]{4,3,2,1,0:T(8,128)(2,1)S(1)}, u32[]{:S(2)}, u32[]{:S(2)}) collective-permute-start(bf16[4,16,2,64,128]{4,3,2,1,0:T(8,128)(2,1)S(1)} %get-tuple-element.8), channel_id=1, source_target_pairs={{0,32},{32,0},{1,33},{33,1},{2,34},{34,2},{3,35},{35,3},{4,36},{36... | collective-permute-start | bytes 6291464 | tf_op jit(solution)/shard_map/ppermute | solution.py:228
  104.4 39.3 %copy-start.1 = (f32[256,256]{1,0:T(8,128)S(1)}, f32[256,256]{1,0:T(8,128)}, u32[]{:S(2)}) copy-start(f32[256,256]{1,0:T(8,128)} %constant.47.clone.turn_ref) | copy-start | bytes 786436
  104.4 39.3 %copy-start.3 = (f32[16,128]{1,0:T(8,128)S(1)}, f32[16,128]{1,0:T(8,128)}, u32[]{:S(2)}) copy-start(f32[16,128]{1,0:T(8,128)} %constant.48.clone.mean_ref) | copy-start | bytes 24580
  104.4 25.0 %collective-permute-start.1 = (bf16[2,8,2,64,128]{4,3,2,1,0:T(8,128)(2,1)S(1)}, bf16[2,8,2,64,128]{4,3,2,1,0:T(8,128)(2,1)S(1)}, u32[]{:S(2)}, u32[]{:S(2)}) collective-permute-start(bf16[2,8,2,64,128]{4,3,2,1,0:T(8,128)(2,1)S(1)} %slice_bitcast_fusion.5), channel_id=1, source_target_pairs={{0,64},{64,0},{128,192},{192,128},{1,65},{65,1},{129,193},{193,129... | collective-permute-start | bytes 1572872 | tf_op jit(solution)/shard_map/ppermute | solution.py:228
  106.6 25.9 %collective-permute-start.3 = (bf16[2,8,2,64,128]{4,3,2,1,0:T(8,128)(2,1)S(1)}, bf16[2,8,2,64,128]{4,3,2,1,0:T(8,128)(2,1)S(1)}, u32[]{:S(2)}, u32[]{:S(2)}) collective-permute-start(bf16[2,8,2,64,128]{4,3,2,1,0:T(8,128)(2,1)S(1)} %slice_bitcast_fusion.3), channel_id=1, source_target_pairs={{0,128},{64,192},{128,0},{192,64},{1,129},{65,193},{129,1},{193,65... | collective-permute-start | bytes 1572872 | tf_op jit(solution)/shard_map/ppermute | solution.py:228
  133.0 10.6 %collective-permute-start.4 = (bf16[8,2,64,128]{3,2,1,0:T(8,128)(2,1)S(1)}, bf16[8,2,64,128]{3,2,1,0:T(8,128)(2,1)S(1)}, u32[]{:S(2)}, u32[]{:S(2)}) collective-permute-start(bf16[8,2,64,128]{3,2,1,0:T(8,128)(2,1)S(1)} %fusion.3), channel_id=1, source_target_pairs={{0,64},{64,0},{128,192},{192,128},{1,65},{65,1},{129,193},{193,129... | collective-permute-start | bytes 786440 | tf_op jit(solution)/shard_map/ppermute | solution.py:228
  133.2 13.6 %collective-permute-start.2 = (bf16[8,2,64,128]{3,2,1,0:T(8,128)(2,1)S(1)}, bf16[8,2,64,128]{3,2,1,0:T(8,128)(2,1)S(1)}, u32[]{:S(2)}, u32[]{:S(2)}) collective-permute-start(bf16[8,2,64,128]{3,2,1,0:T(8,128)(2,1)S(1)} %fusion.2), channel_id=1, source_target_pairs={{0,128},{64,192},{128,0},{192,64},{1,129},{65,193},{129,1},{193,65... | collective-permute-start | bytes 786440 | tf_op jit(solution)/shard_map/ppermute | solution.py:228

commit v2 on v0

v2 whole, which is shorter than its diff:
```python
import functools
import math

import jax
import jax.numpy as jnp
import numpy as np
from jax import lax
from jax.experimental import pallas as pl
from jax.experimental.pallas import tpu as pltpu
from jax.sharding import Mesh
from jax.sharding import PartitionSpec as P

CHAN = 1024
NFFT = 2048
TAPS = 4
UPCH = 16
WIN = 512
SPECTRA = 128
BAND_LO = 256
LANES = 128
OWN = 8
NT = NFFT // LANES
LARGE, SMALL = 60 << 20, 16 << 20
SHORT = pl.CostEstimate(flops=1, bytes_accessed=1, transcendentals=0)


def taper_table():
    index = np.arange(TAPS * NFFT, dtype=np.float64)
    centred = (index - TAPS * NFFT / 2.0 + 0.5) / NFFT
    window = 0.5 - 0.5 * np.cos(2.0 * math.pi * (index + 0.5) / (TAPS * NFFT))
    return (np.sinc(centred) * window).astype(np.float32).reshape(TAPS, NFFT)


def transform_table():
    chan_ids = BAND_LO + np.arange(WIN)
    angles = 2.0 * math.pi * ((chan_ids[:, None] * np.arange(NFFT)[None, :]) % NFFT) / NFFT
    stacked = np.stack([np.cos(angles), -np.sin(angles)], axis=1) / math.sqrt(CHAN)
    return stacked.reshape(2 * WIN, NFFT).astype(jnp.bfloat16)


FIR_BLOCK = 32
HALO = TAPS - 1


def transform_block(table, frames_ref, turn_ref):
    rows = table.shape[0]
    for pair in range(OWN // 2):
        part = lax.dot_general(
            table,
            frames_ref[pl.ds(pair * 2 * SPECTRA, 2 * SPECTRA), :],
            (((1,), (1,)), ((), ())),
            preferred_element_type=jnp.float32,
        )
        for half in range(2):
            turn_ref[pl.ds(pair * 2 + half, rows, stride=OWN), :] = part[:, half * SPECTRA : (half + 1) * SPECTRA]


PLANE = 16


def place(turn_ref, out_ref, mine):
    rows = turn_ref.shape[0] // PLANE
    for owner in range(PLANE):
        out_ref[mine ^ owner] = turn_ref[owner * rows : (owner + 1) * rows, :].astype(jnp.bfloat16)


def channelize_kernel(
    where_ref, volts_hbm, taper_ref, table_hbm, first_hbm, rest_hbm,
    volts_ref, table_ref, frames_ref, turn_ref, first_ref, rest_ref, sems,
):
    blocks = SPECTRA // FIR_BLOCK
    copies = []
    for block in range(blocks):
        first = block * FIR_BLOCK + (HALO if block else 0)
        last = (block + 1) * FIR_BLOCK + HALO
        span = pl.ds(first * NFFT, (last - first) * NFFT)
        copies.append(pltpu.make_async_copy(volts_hbm.at[:, span], volts_ref.at[:, span], sems.at[block]))
        copies[-1].start()
    table_copy = pltpu.make_async_copy(table_hbm, table_ref, sems.at[blocks])
    table_copy.start()

    for block in range(blocks):
        copies[block].wait()

        def fir_tile(nt, _, block=block):
            lane = pl.multiple_of(nt * LANES, LANES)
            taps = [taper_ref[t, :, pl.ds(lane, LANES)] for t in range(TAPS)]

            def load(frame):
                at = pl.multiple_of((block * FIR_BLOCK + frame) * NFFT + lane, LANES)
                return volts_ref[:, pl.ds(at, LANES)].astype(jnp.float32)

            held = [load(t) for t in range(HALO)]
            done = []
            for s in range(FIR_BLOCK):
                held.append(load(s + HALO))
                total = taps[0] * held[0]
                for t in range(1, TAPS):
                    total = total + taps[t] * held[t]
                held = held[1:]
                done.append(total)
            turned = jnp.swapaxes(jnp.stack(done, axis=0), 0, 1).astype(jnp.bfloat16)
            for i in range(OWN):
                frames_ref[pl.ds(i * SPECTRA + block * FIR_BLOCK, FIR_BLOCK), pl.ds(lane, LANES)] = turned[i]
            return 0

        lax.fori_loop(0, NT, fir_tile, 0)
    table_copy.wait()
    far, near = 1 - where_ref[0], where_ref[0]
    transform_block(table_ref[far, 0], frames_ref, turn_ref)
    place(turn_ref, first_ref, where_ref[1])
    copies = [pltpu.make_async_copy(first_ref, first_hbm, sems.at[blocks + 1])]
    copies[0].start()
    sent = first_ref.shape[1]
    for part, (plane, chunk) in enumerate(((far, 1), (near, 0), (near, 1))):
        transform_block(table_ref[plane, chunk], frames_ref, turn_ref)
        rows = pl.ds(part * sent, sent)
        place(turn_ref, rest_ref.at[:, rows, :], 0)
        copies.append(
            pltpu.make_async_copy(rest_ref.at[:, rows, :], rest_hbm.at[:, rows, :], sems.at[blocks + 2 + part])
        )
        copies[-1].start()
    for copy in copies:
        copy.wait()


def channelize(where, volts, table):
    taper = jnp.asarray(np.broadcast_to(taper_table()[:, None, :], (TAPS, OWN, NFFT)).copy())
    sent = table.shape[2] * OWN // PLANE
    first = jax.ShapeDtypeStruct((PLANE, sent, SPECTRA), jnp.bfloat16)
    rest = jax.ShapeDtypeStruct((PLANE, 3 * sent, SPECTRA), jnp.bfloat16)
    vmem, hbm = pl.BlockSpec(memory_space=pltpu.VMEM), pl.BlockSpec(memory_space=pl.ANY)
    return pl.pallas_call(
        channelize_kernel,
        out_shape=(first, rest),
        in_specs=[pl.BlockSpec(memory_space=pltpu.SMEM), hbm, vmem, hbm],
        out_specs=(hbm, hbm),
        scratch_shapes=[
            pltpu.VMEM(volts.shape, jnp.bfloat16),
            pltpu.VMEM(table.shape, jnp.bfloat16),
            pltpu.VMEM((SPECTRA * OWN, NFFT), jnp.bfloat16),
            pltpu.VMEM((table.shape[2] * OWN, SPECTRA), jnp.float32),
            pltpu.VMEM(first.shape, jnp.bfloat16),
            pltpu.VMEM(rest.shape, jnp.bfloat16),
            pltpu.SemaphoreType.DMA((SPECTRA // FIR_BLOCK + 5,)),
        ],
        compiler_params=pltpu.CompilerParams(vmem_limit_bytes=LARGE),
        cost_estimate=SHORT,
    )(where, volts, taper, table)


def one_hot(rows, columns):
    return jnp.where(rows == columns, 1.0, 0.0).astype(jnp.bfloat16)


def weight_kernel(swapped, where_ref, order_ref, map_ref, weights_ref, out_ref, pick_ref, place_ref):
    beams = weights_ref.shape[2]
    feeds = weights_ref.shape[3]
    z_hi, y_x, core, z_lo = (where_ref[k] for k in range(4))

    def iota(rows, columns, axis):
        return lax.broadcasted_iota(jnp.int32, (rows, columns), axis)

    def product(one, two, contract):
        return lax.dot_general(
            one, two, (((1,), (contract,)), ((), ())), preferred_element_type=jnp.float32
        ).astype(jnp.bfloat16)

    @pl.when(pl.program_id(0) == 0)
    def _():
        own = beams // 8
        block = iota(beams, beams, 0) // own
        position = ((block % 4) ^ z_lo) * 2 + ((block // 4) ^ core)
        position = position * own + iota(beams, beams, 0) % own
        chosen = one_hot(position, iota(beams, beams, 1))
        pick_ref[...] = product(chosen, one_hot(iota(beams, beams, 0), order_ref[...]), 1)
        at = iota(feeds, 2 * feeds, 1)
        entry = at // (2 * OWN) % PLANE
        is_imag = at // OWN % 2
        feed_of = one_hot(iota(feeds, feeds, 0), map_ref[...])
        y, x = entry // 4, entry % 4
        if swapped:
            far = at // feeds
            y, x = jnp.where(far == 1, entry % 4 ^ y_x // 4, y), jnp.where(far == 1, entry // 4 ^ y_x % 4, x)
        source = y * 8 + (at // feeds ^ z_hi) * 4 + x
        match = product(feed_of, one_hot(iota(feeds, 2 * feeds, 0), source * OWN + at % OWN), 0)
        place_ref[0:feeds] = jnp.where(is_imag == 0, match, jnp.zeros_like(match))
        place_ref[feeds:] = jnp.where(is_imag == 1, match, jnp.zeros_like(match))

    wide = jnp.concatenate([weights_ref[0, 0], weights_ref[0, 1]], axis=1)
    picked = product(pick_ref[...], wide, 0)
    out_ref[0] = product(picked, place_ref[...], 0)


def arrange_weights(where, weights, order, inputs_map, chunk):
    chans, _, beams, feeds = weights.shape
    chans //= 2
    return pl.pallas_call(
        functools.partial(weight_kernel, chunk == 0),
        grid_spec=pltpu.PrefetchScalarGridSpec(
            num_scalar_prefetch=1,
            grid=(chans,),
            in_specs=[
                pl.BlockSpec((1, beams), lambda c, w: (0, 0)),
                pl.BlockSpec((1, feeds), lambda c, w: (0, 0)),
                pl.BlockSpec((1, 2, beams, feeds), lambda c, w: (chunk * chans + c, 0, 0, 0)),
            ],
            out_specs=pl.BlockSpec((1, beams, 2 * feeds), lambda c, w: (c, 0, 0)),
            scratch_shapes=[
                pltpu.VMEM((beams, beams), jnp.bfloat16),
                pltpu.VMEM((2 * feeds, 2 * feeds), jnp.bfloat16),
            ],
        ),
        out_shape=jax.ShapeDtypeStruct((chans, beams, 2 * feeds), jnp.bfloat16),
        compiler_params=pltpu.CompilerParams(vmem_limit_bytes=SMALL),
        cost_estimate=SHORT,
    )(where, order.reshape(1, beams), inputs_map.reshape(1, feeds), weights)


def combine_kernel(turned, weights_ref, near_ref, far_ref, keep_ref, send_ref):
    beams = weights_ref.shape[1]
    spectra = near_ref.shape[3]
    half = beams // 2
    data = jnp.concatenate([near_ref[:, 0], far_ref[:, 0]], axis=0).astype(jnp.float32)
    real, imag = data[:, :OWN], data[:, OWN:]
    of_real = jnp.concatenate([real, -imag], axis=1).reshape(-1, spectra)
    of_imag = jnp.concatenate([imag, real], axis=1).reshape(-1, spectra)
    both = jnp.concatenate([of_real, of_imag], axis=1).astype(jnp.bfloat16)
    product = jnp.dot(weights_ref[0], both, preferred_element_type=jnp.float32)
    for part in range(2):
        mine = product[:, part * spectra : (part + 1) * spectra]
        quarter = half // 4
        for block in range(4):
            at = (block % 2, block // 2) if turned else (block // 2, block % 2)
            rows = slice(block * quarter, (block + 1) * quarter)
            keep_ref[at[0], at[1], 0, part] = mine[:half][rows]
            send_ref[at[0], at[1], 0, part] = mine[half:][rows].astype(jnp.bfloat16)


def combine(arranged, near, near_from, far, chunk):
    beams, wide = arranged.shape[1:]
    sources, chans, rows, spectra = far.shape
    shape = (2, 2, chans, 2, beams // 8, spectra)
    block = pl.BlockSpec((2, 2, 1, 2, beams // 8, spectra), lambda c: (0, 0, c, 0, 0, 0))
    return pl.pallas_call(
        functools.partial(combine_kernel, chunk == 1),
        grid=(chans,),
        out_shape=(jax.ShapeDtypeStruct(shape, jnp.float32), jax.ShapeDtypeStruct(shape, jnp.bfloat16)),
        in_specs=[
            pl.BlockSpec((1, beams, wide), lambda c: (c, 0, 0)),
            pl.BlockSpec((sources, 1, rows, spectra), lambda c: (0, near_from + c, 0, 0)),
            pl.BlockSpec((sources, 1, rows, spectra), lambda c: (0, c, 0, 0)),
        ],
        out_specs=(block, block),
        compiler_params=pltpu.CompilerParams(vmem_limit_bytes=SMALL),
        cost_estimate=SHORT,
    )(arranged, near, far)


def fine_tables():
    steps = np.arange(UPCH)
    angles = 2.0 * math.pi * (np.outer(steps, steps) % UPCH) / UPCH
    eye = np.eye(SPECTRA // UPCH)
    real = np.kron(eye, np.cos(angles) / math.sqrt(UPCH))
    imag = np.kron(eye, -np.sin(angles) / math.sqrt(UPCH))
    turn = np.block([[real, imag], [-imag, real]]).astype(np.float32)
    mean = np.tile(np.eye(UPCH) * UPCH / SPECTRA, (1, SPECTRA // UPCH)).astype(np.float32)
    high = turn.astype(jnp.bfloat16)
    low = (turn - high.astype(np.float32)).astype(jnp.bfloat16)
    return np.stack([high, low]), mean


def three_products(value, high, low):
    top = value.astype(jnp.bfloat16)
    rest = (value - top.astype(jnp.float32)).astype(jnp.bfloat16)
    wide = jnp.float32
    total = jnp.dot(top, low, preferred_element_type=wide) + jnp.dot(rest, high, preferred_element_type=wide)
    return total + jnp.dot(top, high, preferred_element_type=wide)


def detect_kernel(*refs):
    halves, (turn_ref, mean_ref, out_ref) = refs[:-3], refs[-3:]
    wide = jnp.float32
    for at in range(0, len(halves), 4):
        keep_ref, come_ref, one_ref, two_ref = halves[at : at + 4]
        total = keep_ref[0, 0] + come_ref[0, 0].astype(wide) + one_ref[0].astype(wide) + two_ref[...].astype(wide)
        chans, _, beams, spectra = total.shape
        both = jnp.concatenate(
            [total[:, 0].reshape(chans * beams, spectra), total[:, 1].reshape(chans * beams, spectra)], axis=1
        )
        sub = three_products(both, turn_ref[0], turn_ref[1])
        power = sub[:, :spectra] * sub[:, :spectra] + sub[:, spectra:] * sub[:, spectra:]
        mean = lax.dot_general(
            mean_ref[...], power, (((1,), (1,)), ((), ())), preferred_element_type=wide, precision=lax.Precision.HIGHEST
        )
        for chan in range(chans):
            out_ref[at // 4 * chans + chan] = mean[:, chan * beams : (chan + 1) * beams]


def detect(halves):
    chans, _, beams, spectra = halves[0][0].shape[2:]
    turn, mean = fine_tables()
    block = (chans, 2, beams, spectra)
    corner = pl.BlockSpec((1, 1) + block, lambda k: (0,) * 6)
    one = pl.BlockSpec((1,) + block, lambda k: (0,) * 5)
    two = pl.BlockSpec(block, lambda k: (0,) * 4)
    whole = pl.BlockSpec(memory_space=pltpu.VMEM)
    return pl.pallas_call(
        detect_kernel,
        grid=(1,),
        out_shape=jax.ShapeDtypeStruct((len(halves) * chans, UPCH, beams), jnp.float32),
        in_specs=[corner, corner, one, two] * len(halves) + [whole] * 2,
        out_specs=whole,
        compiler_params=pltpu.CompilerParams(vmem_limit_bytes=SMALL),
        cost_estimate=SHORT,
    )(*[part for half in halves for part in half], jnp.asarray(turn), jnp.asarray(mean))


def swap(value, axis, distance, size):
    return lax.ppermute(value, axis, [(k, k ^ distance) for k in range(size)])


def after(value, earlier):
    return lax.optimization_barrier((value, earlier))[0]


def narrow(value):
    return value.astype(jnp.bfloat16)


def widen(value):
    return value.astype(jnp.float32)


def channel_table(chans):
    rows = transform_table().reshape(4, 2, 4, 2, chans, NFFT)
    return jnp.asarray(np.transpose(rows, (1, 3, 0, 2, 4, 5)).reshape(2, 2, 16 * chans, NFFT))


def on_device(voltages, weights, input_map, beam_order):
    chans = weights.shape[0]
    half = chans // 2
    table = channel_table(chans)
    z_hi = lax.axis_index("zh")
    y, x = lax.axis_index("y"), lax.axis_index("x")
    core, z = lax.axis_index("core"), lax.axis_index("zl")
    where = jnp.stack([z_hi, 4 * y + x, core, z]).astype(jnp.int32)

    def turn_by_swaps(value):
        value = value.reshape(4, 4, -1, SPECTRA)
        rows = [value[0]] + [swap(value[k], "y", k, 4) for k in (1, 2, 3)]
        columns = [jnp.stack([row[k] for row in rows]) for k in range(4)]
        columns = [columns[0]] + [swap(columns[k], "x", k, 4) for k in (1, 2, 3)]
        return jnp.stack(columns).reshape(PLANE, -1, 2 * OWN, SPECTRA)

    def turn(value):
        value = lax.all_to_all(value.reshape(PLANE, -1, SPECTRA), ("y", "x"), split_axis=0, concat_axis=0, tiled=True)
        return value.reshape(PLANE, -1, 2 * OWN, SPECTRA)

    first, rest = channelize(where, voltages, table)
    far0 = swap(first, "zh", 1, 2)
    planed = turn(rest)
    far1 = swap(planed[:, :half], "zh", 1, 2)
    arranged0 = arrange_weights(where, after(weights, rest), beam_order, input_map, 0)
    arranged1 = arrange_weights(where, after(after(weights, planed), arranged0), beam_order, input_map, 1)
    data0 = after(turn_by_swaps(after(far0, arranged1)), far1)

    keep0, send0 = combine(arranged0, planed, half, data0, 0)
    come0 = swap(send0, "core", 1, 2)
    to0 = narrow(keep0[1] + widen(come0[1]))
    keep1, send1 = combine(arranged1, planed, 2 * half, far1, 1)
    come1 = swap(send1, "core", 1, 2)
    one0 = swap(to0, "zl", 2, 4)
    one1 = swap(narrow(keep1[1] + widen(come1[1])), "zl", 1, 4)
    two0 = swap(narrow(keep0[0, 1] + widen(come0[0, 1]) + widen(one0[1])), "zl", 1, 4)
    two1 = swap(narrow(keep1[0, 1] + widen(come1[0, 1]) + widen(one1[1])), "zl", 2, 4)
    return detect([(keep0, come0, one0, two0), (keep1, come1, one1, two1)])


def solution(mesh):
    fine = Mesh(mesh.devices.reshape(4, 2, 4, 2, 4), ("zl", "core", "y", "zh", "x"))
    grp, dev = ("zl", "core"), ("y", "zh", "x")
    placed = (P(grp + dev, None), P(dev, None, None, grp), P(grp), P())
    return jax.shard_map(on_device, mesh=fine, in_specs=placed, out_specs=P(dev, None, grp), check_vma=False)
```

time: 334 us -> 130 us (0.39); the launches traced: 327 us -> 130 us
  local copies, waits for them, and re-layouts: 86.4 us -> 8.85 us
  matrix products: 72.4 us -> 0 us
  waiting for transfers between devices: 107 us -> 49.4 us
  Pallas kernels: 0 us -> 34.1 us
  other arithmetic: 33.6 us -> 1.27 us
  starting transfers between devices: 14.3 us -> 35.8 us
  between operations: 14.1 us -> 0.26 us
    reduce_scatter x1 -> x0, waiting for transfers between devices: 90.2 us -> none  [on_device(): lax.psum_scatter(combine(ordered, local_data), 'grp', scatter_dimension=0...]
    dot_general x6 -> x0, matrix products: 72.4 us -> none  [the longest x1 54.9 us: channelize(): jnp.einsum('kn,isn->ksi', transform_table(chan, first, count), summed, pr...]
    ppermute x0 -> x14, waiting for transfers between devices: none -> 47.5 us  [swap(): return lax.ppermute(value, axis, [(k, k ^ distance) for k in range(size)])]
    gather x2 -> x0, local copies, waits for them, and re-layouts: 37.6 us -> none  [the longest x1 35 us: on_device(): ordered = jnp.take(weights, beam_order, axis=2)]
    pallas_call x0 -> x6, Pallas kernels: none -> 34.1 us  [the longest x2 13.9 us: arrange_weights(): pl.pallas_call(functools.partial(weight_kernel, chunk == 0), grid_spec=pl...]
    ppermute x0 -> x14, starting transfers between devices: none -> 28.2 us  [swap(): return lax.ppermute(value, axis, [(k, k ^ distance) for k in range(size)])]
    another operation x3 -> x6, other arithmetic: 22.8 us -> 0.76 us  [the longest x1 0.61 us: on_device(): where = jnp.stack([z_hi, 4 * y + x, core, z]).astype(jnp.int32)]
    another operation x2 -> x0, local copies, waits for them, and re-layouts: 16.8 us -> none  [the longest x1 10.5 us: combine(): return jnp.stack([real_part, imag_part], axis=2)]
  transfers between devices with their start and end apart: 2 -> 15, of which waited for: 2 -> 11; matrix products, arithmetic and copies ran while one was open for 11% -> 1% of each run, Pallas kernels for 0% -> 13%
where the time goes in v2:
time: 130 us
  waiting for transfers between devices  49.4 us (38%)
  starting transfers between devices  35.8 us (28%)
  Pallas kernels  34.1 us (26%)
  local copies, waits for them, and re-layouts  8.85 us (7%)
    ppermute x14, waiting for transfers between devices, swap(): return lax.ppermute(value, axis, [(k, k ^ distance) for k in range(size)])  47.5 us
    ppermute x14, starting transfers between devices, swap(): return lax.ppermute(value, axis, [(k, k ^ distance) for k in range(size)])  28.2 us
    pallas_call x2, Pallas kernels, arrange_weights(): pl.pallas_call(functools.partial(weight_kernel, chunk == 0), grid_spec=pl...  13.9 us
    pallas_call x1, Pallas kernels, channelize(): pl.pallas_call(channelize_kernel, out_shape=(first, rest), in_specs=[pl.B...  12.4 us
    unnamed x20, local copies, waits for them, and re-layouts  8.74 us
    all_to_all x1, starting transfers between devices, turn(): lax.all_to_all(value.reshape(PLANE, -1, SPECTRA), ('y', 'x'), split_axis=...  7.62 us
    pallas_call x2, Pallas kernels, combine(): pl.pallas_call(functools.partial(combine_kernel, chunk == 1), grid=(chans...  5.58 us
  transfers between devices with their start and end apart: 15, of which 11 were waited for; matrix products, arithmetic and copies ran while one was open for 1% of the time, Pallas kernels for 13%

profile of v2, /device:TPU:2, one launch (start us, length us, event | category | flops | bytes accessed | tf_op | source)
XLA Modules:
  0.0 129.6 jit_solution(8597285294061685618)
XLA Ops:
  0.0 0.6 pad_add_fusion.where_ref
  0.6 12.4 %shard_map.82 = (bf16[16,128,128]{2,1,0:T(8,128)(2,1)}, bf16[16,384,128]{2,1,0:T(8,128)(2,1)}) custom-call(s32[4]{0:T(128)} %pad_add_fusion.where_ref, bf16[8,268288]{1,0:T(8,128)(2,1)} %volts_hbm.1, f32[4,8,2048]{2,1,0:T(8,128)} %constant.31.clone.taper_ref, bf16[2,2,256,2048]{3,2,1,0:T(8,128)(2,1)} %constant.30.clone.table_hbm), custom_call_target="tpu_custom_call" | custom-call | flops 1 | bytes 1 | tf_op jit(solution)/shard_map/pallas_call | solution.py:133
  13.0 0.0 copy-start.9
  13.1 0.0 copy-start.6
  13.1 0.0 copy-start.7
  13.1 0.0 copy-start.8
  13.1 7.6 %all-to-all-start = ((bf16[16,384,128]{2,1,0:T(8,128)(2,1)}), bf16[16,384,128]{2,1,0:T(8,128)(2,1)S(1)}, u32[]{:S(2)}, u32[]{:S(2)}) async-start(bf16[16,384,128]{2,1,0:T(8,128)(2,1)} %get-tuple-element.16), calls=%async_computation | async-start | bytes 3145728 | tf_op jit(solution)/shard_map/all_to_all | solution.py:357
  20.7 0.0 copy-done.9
  20.7 7.3 %collective-permute-start = (bf16[16,128,128]{2,1,0:T(8,128)(2,1)S(1)}, bf16[16,128,128]{2,1,0:T(8,128)(2,1)S(1)}, u32[]{:S(2)}, u32[]{:S(2)}) collective-permute-start(bf16[16,128,128]{2,1,0:T(8,128)(2,1)S(1)} %copy-done.9), channel_id=1, source_target_pairs={{0,4},{4,0},{1,5},{5,1},{2,6},{6,2},{3,7},{7,3},{8,12},{12,8},{9,1... | collective-permute-start | bytes 1572872 | tf_op jit(solution)/shard_map/ppermute | solution.py:320
  28.0 0.0 copy-done.6
  28.0 0.0 copy-done.7
  28.0 0.0 copy-done.8
  28.0 0.0 copy-start
  28.0 3.4 %copy-done = bf16[16,2,512,256]{3,2,1,0:T(8,128)(2,1)S(1)} copy-done((bf16[16,2,512,256]{3,2,1,0:T(8,128)(2,1)S(1)}, bf16[16,2,512,256]{3,2,1,0:T(8,128)(2,1)}, u32[]{:S(2)}) %copy-start) | copy-done | bytes 8388632
  31.4 7.0 %shard_map.83.weights_ref = bf16[8,512,512]{2,1,0:T(8,128)(2,1)S(1)} custom-call(s32[4]{0:T(128)S(1)} %copy-done.6, s32[1,512]{1,0:T(1,128)S(1)} %bitcast.35, s32[1,256]{1,0:T(1,128)S(1)} %bitcast.37, bf16[16,2,512,256]{3,2,1,0:T(8,128)(2,1)S(1)} %copy-done), custom_call_target="tpu_custom_call" | custom-call | flops 1 | bytes 1 | tf_op jit(solution)/shard_map/pallas_call | solution.py:198
  38.4 0.0 copy-start.2
  38.4 1.9 %copy-done.2 = bf16[8,512,512]{2,1,0:T(8,128)(2,1)} copy-done((bf16[8,512,512]{2,1,0:T(8,128)(2,1)}, bf16[8,512,512]{2,1,0:T(8,128)(2,1)S(1)}, u32[]{:S(2)}) %copy-start.2) | copy-done | bytes 4194328
  40.3 1.9 %all-to-all-done = bf16[16,384,128]{2,1,0:T(8,128)(2,1)S(1)} async-done(((bf16[16,384,128]{2,1,0:T(8,128)(2,1)}), bf16[16,384,128]{2,1,0:T(8,128)(2,1)S(1)}, u32[]{:S(2)}, u32[]{:S(2)}) %all-to-all-start) | async-done | bytes 1572896 | tf_op jit(solution)/shard_map/all_to_all | solution.py:357
  42.3 7.3 %collective-permute-start.7 = (bf16[16,8,16,128]{3,2,1,0:T(8,128)(2,1)S(1)}, bf16[16,8,16,128]{3,2,1,0:T(8,128)(2,1)S(1)}, u32[]{:S(2)}, u32[]{:S(2)}) collective-permute-start(bf16[16,8,16,128]{3,2,1,0:T(8,128)(2,1)S(1)} %slice.142), channel_id=1, source_target_pairs={{0,4},{4,0},{1,5},{5,1},{2,6},{6,2},{3,7},{7,3},{8,12},{12,8},{9,1... | collective-permute-start | bytes 1572872 | tf_op jit(solution)/shard_map/ppermute | solution.py:320
  49.5 0.0 copy-start.1
  49.5 3.4 %copy-done.1 = bf16[16,2,512,256]{3,2,1,0:T(8,128)(2,1)S(1)} copy-done((bf16[16,2,512,256]{3,2,1,0:T(8,128)(2,1)S(1)}, bf16[16,2,512,256]{3,2,1,0:T(8,128)(2,1)}, u32[]{:S(2)}) %copy-start.1) | copy-done | bytes 8388632
  52.9 0.0 copy-start.3
  52.9 7.0 %shard_map.84.weights_ref = bf16[8,512,512]{2,1,0:T(8,128)(2,1)S(1)} custom-call(s32[4]{0:T(128)S(1)} %copy-done.6, s32[1,512]{1,0:T(1,128)S(1)} %bitcast.36, s32[1,256]{1,0:T(1,128)S(1)} %bitcast.38, bf16[16,2,512,256]{3,2,1,0:T(8,128)(2,1)S(1)} %copy-done.1), custom_call_target="tpu_custom_call" | custom-call | flops 1 | bytes 1 | tf_op jit(solution)/shard_map/pallas_call | solution.py:198
  59.9 0.0 collective-permute-done
  59.9 0.1 collective-permute-start.1
  60.0 1.4 %collective-permute-start.3 = (bf16[4,128,128]{2,1,0:T(8,128)(2,1)S(1)}, bf16[4,128,128]{2,1,0:T(8,128)(2,1)S(1)}, u32[]{:S(2)}, u32[]{:S(2)}) collective-permute-start(bf16[4,128,128]{2,1,0:T(8,128)(2,1)S(1)} %get-tuple-element.32), channel_id=1, source_target_pairs={{0,24},{8,16},{16,8},{24,0},{1,25},{9,17},{17,9},{25,1},{2,26},{10... | collective-permute-start | bytes 393224 | tf_op jit(solution)/shard_map/ppermute | solution.py:320
  61.4 2.7 %collective-permute-start.2 = (bf16[4,128,128]{2,1,0:T(8,128)(2,1)S(1)}, bf16[4,128,128]{2,1,0:T(8,128)(2,1)S(1)}, u32[]{:S(2)}, u32[]{:S(2)}) collective-permute-start(bf16[4,128,128]{2,1,0:T(8,128)(2,1)S(1)} %get-tuple-element.33), channel_id=1, source_target_pairs={{0,16},{8,24},{16,0},{24,8},{1,17},{9,25},{17,1},{25,9},{2,18},{10... | collective-permute-start | bytes 393224 | tf_op jit(solution)/shard_map/ppermute | solution.py:320
  64.1 1.5 %collective-permute-done.1 = bf16[4,128,128]{2,1,0:T(8,128)(2,1)S(1)} collective-permute-done((bf16[4,128,128]{2,1,0:T(8,128)(2,1)S(1)}, bf16[4,128,128]{2,1,0:T(8,128)(2,1)S(1)}, u32[]{:S(2)}, u32[]{:S(2)}) %collective-permute-start.1) | collective-permute-done | bytes 131104 | tf_op jit(solution)/shard_map/ppermute | solution.py:320
  65.6 3.2 %collective-permute-done.3 = bf16[4,128,128]{2,1,0:T(8,128)(2,1)S(1)} collective-permute-done((bf16[4,128,128]{2,1,0:T(8,128)(2,1)S(1)}, bf16[4,128,128]{2,1,0:T(8,128)(2,1)S(1)}, u32[]{:S(2)}, u32[]{:S(2)}) %collective-permute-start.3) | collective-permute-done | bytes 131104 | tf_op jit(solution)/shard_map/ppermute | solution.py:320
  68.8 0.0 collective-permute-done.2
  68.9 2.3 %collective-permute-start.4 = (bf16[4,128,128]{2,1,0:T(8,128)(2,1)S(1)}, bf16[4,128,128]{2,1,0:T(8,128)(2,1)S(1)}, u32[]{:S(2)}, u32[]{:S(2)}) collective-permute-start(bf16[4,128,128]{2,1,0:T(8,128)(2,1)S(1)} %pad_maximum_fusion.1), channel_id=1, source_target_pairs={{0,1},{1,0},{2,3},{3,2},{4,5},{5,4},{6,7},{7,6},{8,9},{9,8},{10,11... | collective-permute-start | bytes 393224 | tf_op jit(solution)/shard_map/ppermute | solution.py:320
  71.2 1.8 %collective-permute-start.5 = (bf16[4,128,128]{2,1,0:T(8,128)(2,1)S(1)}, bf16[4,128,128]{2,1,0:T(8,128)(2,1)S(1)}, u32[]{:S(2)}, u32[]{:S(2)}) collective-permute-start(bf16[4,128,128]{2,1,0:T(8,128)(2,1)S(1)} %pad_maximum_fusion.2), channel_id=1, source_target_pairs={{0,2},{1,3},{2,0},{3,1},{4,6},{5,7},{6,4},{7,5},{8,10},{9,11},{10,... | collective-permute-start | bytes 393224 | tf_op jit(solution)/shard_map/ppermute | solution.py:320
  73.0 0.3 collective-permute-start.6
  73.3 1.6 %collective-permute-done.4 = bf16[4,128,128]{2,1,0:T(8,128)(2,1)S(1)} collective-permute-done((bf16[4,128,128]{2,1,0:T(8,128)(2,1)S(1)}, bf16[4,128,128]{2,1,0:T(8,128)(2,1)S(1)}, u32[]{:S(2)}, u32[]{:S(2)}) %collective-permute-start.4) | collective-permute-done | bytes 131104 | tf_op jit(solution)/shard_map/ppermute | solution.py:320
  74.9 3.0 %collective-permute-done.5 = bf16[4,128,128]{2,1,0:T(8,128)(2,1)S(1)} collective-permute-done((bf16[4,128,128]{2,1,0:T(8,128)(2,1)S(1)}, bf16[4,128,128]{2,1,0:T(8,128)(2,1)S(1)}, u32[]{:S(2)}, u32[]{:S(2)}) %collective-permute-start.5) | collective-permute-done | bytes 131104 | tf_op jit(solution)/shard_map/ppermute | solution.py:320
  77.8 1.3 %collective-permute-done.6 = bf16[4,128,128]{2,1,0:T(8,128)(2,1)S(1)} collective-permute-done((bf16[4,128,128]{2,1,0:T(8,128)(2,1)S(1)}, bf16[4,128,128]{2,1,0:T(8,128)(2,1)S(1)}, u32[]{:S(2)}, u32[]{:S(2)}) %collective-permute-start.6) | collective-permute-done | bytes 131104 | tf_op jit(solution)/shard_map/ppermute | solution.py:320
  79.2 0.1 pad_maximum_fusion
  79.2 0.0 collective-permute-done.7.far_ref
  79.2 0.0 copy-done.3
  79.2 2.8 %shard_map.85 = (f32[2,2,8,2,64,128]{5,4,3,2,1,0:T(8,128)S(1)}, bf16[2,2,8,2,64,128]{5,4,3,2,1,0:T(8,128)(2,1)S(1)}) custom-call(bf16[8,512,512]{2,1,0:T(8,128)(2,1)S(1)} %copy-done.3, bf16[16,24,16,128]{3,2,1,0:T(8,128)(2,1)S(1)} %bitcast.32, bf16[16,8,16,128]{3,2,1,0:T(8,128)(2,1)S(1)} %bitcast.34), custom_call_target="tpu_custom_call" | custom-call | flops 1 | bytes 1 | tf_op jit(solution)/shard_map/pallas_call | solution.py:245
  82.1 0.1 collective-permute-start.8
  82.2 2.8 %shard_map.86 = (f32[2,2,8,2,64,128]{5,4,3,2,1,0:T(8,128)S(1)}, bf16[2,2,8,2,64,128]{5,4,3,2,1,0:T(8,128)(2,1)S(1)}) custom-call(bf16[8,512,512]{2,1,0:T(8,128)(2,1)S(1)} %shard_map.84.weights_ref, bf16[16,24,16,128]{3,2,1,0:T(8,128)(2,1)S(1)} %bitcast.33, bf16[16,8,16,128]{3,2,1,0:T(8,128)(2,1)S(1)} %collective-permute-done.7.far_ref), custom_call_target="tpu_custom_call" | custom-call | flops 1 | bytes 1 | tf_op jit(solution)/shard_map/pallas_call | solution.py:245
  84.9 0.6 collective-permute-start.11
  85.5 0.0 collective-permute-done.8.refs_1_
  85.5 0.2 fusion
  85.7 1.5 %collective-permute-start.9 = (bf16[2,8,2,64,128]{4,3,2,1,0:T(8,128)(2,1)S(1)}, bf16[2,8,2,64,128]{4,3,2,1,0:T(8,128)(2,1)S(1)}, u32[]{:S(2)}, u32[]{:S(2)}) collective-permute-start(bf16[2,8,2,64,128]{4,3,2,1,0:T(8,128)(2,1)S(1)} %fusion), channel_id=1, source_target_pairs={{0,128},{64,192},{128,0},{192,64},{1,129},{65,193},{129,1},{193,65... | collective-permute-start | bytes 1572872 | tf_op jit(solution)/shard_map/ppermute | solution.py:320
  87.2 0.6 collective-permute-done.11.refs_5_
  87.8 0.0 copy-start.4
  87.8 0.0 copy-start.5
  87.8 0.1 fusion.1
  88.0 1.1 collective-permute-start.12
  89.1 22.8 %collective-permute-done.9.refs_2_ = bf16[2,8,2,64,128]{4,3,2,1,0:T(8,128)(2,1)S(1)} collective-permute-done((bf16[2,8,2,64,128]{4,3,2,1,0:T(8,128)(2,1)S(1)}, bf16[2,8,2,64,128]{4,3,2,1,0:T(8,128)(2,1)S(1)}, u32[]{:S(2)}, u32[]{:S(2)}) %collective-permute-start.9) | collective-permute-done | bytes 524320 | tf_op jit(solution)/shard_map/ppermute | solution.py:320
  111.9 0.1 fusion.3
  112.0 0.1 collective-permute-start.10
  112.1 0.9 collective-permute-done.12.refs_6_
  113.0 0.1 fusion.2
  113.1 1.7 %collective-permute-start.13 = (bf16[8,2,64,128]{3,2,1,0:T(8,128)(2,1)S(1)}, bf16[8,2,64,128]{3,2,1,0:T(8,128)(2,1)S(1)}, u32[]{:S(2)}, u32[]{:S(2)}) collective-permute-start(bf16[8,2,64,128]{3,2,1,0:T(8,128)(2,1)S(1)} %fusion.2), channel_id=1, source_target_pairs={{0,128},{64,192},{128,0},{192,64},{1,129},{65,193},{129,1},{193,65... | collective-permute-start | bytes 786440 | tf_op jit(solution)/shard_map/ppermute | solution.py:320
  114.8 8.9 %collective-permute-done.10.refs_3_ = bf16[8,2,64,128]{3,2,1,0:T(8,128)(2,1)S(1)} collective-permute-done((bf16[8,2,64,128]{3,2,1,0:T(8,128)(2,1)S(1)}, bf16[8,2,64,128]{3,2,1,0:T(8,128)(2,1)S(1)}, u32[]{:S(2)}, u32[]{:S(2)}) %collective-permute-start.10) | collective-permute-done | bytes 262176 | tf_op jit(solution)/shard_map/ppermute | solution.py:320
  123.7 3.8 %collective-permute-done.13.refs_7_ = bf16[8,2,64,128]{3,2,1,0:T(8,128)(2,1)S(1)} collective-permute-done((bf16[8,2,64,128]{3,2,1,0:T(8,128)(2,1)S(1)}, bf16[8,2,64,128]{3,2,1,0:T(8,128)(2,1)S(1)}, u32[]{:S(2)}, u32[]{:S(2)}) %collective-permute-start.13) | collective-permute-done | bytes 262176 | tf_op jit(solution)/shard_map/ppermute | solution.py:320
  127.5 0.0 copy-done.4
  127.5 0.0 copy-done.5
  127.5 2.1 %shard_map.87 = f32[16,16,64]{2,1,0:T(8,128)} custom-call(f32[2,2,8,2,64,128]{5,4,3,2,1,0:T(8,128)S(1)} %get-tuple-element.23.refs_0_, bf16[2,2,8,2,64,128]{5,4,3,2,1,0:T(8,128)(2,1)S(1)} %collective-permute-done.8.refs_1_, bf16[2,8,2,64,128]{4,3,2,1,0:T(8,128)(2,1)S(1)} %collective-permute-done.9.refs_2_, ...), custom_call_target="tpu_custom_call" | custom-call | flops 1 | bytes 1 | tf_op jit(solution)/shard_map/pallas_call | solution.py:308
  (10 shorter events, 0.2 us)
Async XLA Ops:
  13.0 7.7 %copy-start.9 = (bf16[16,128,128]{2,1,0:T(8,128)(2,1)S(1)}, bf16[16,128,128]{2,1,0:T(8,128)(2,1)}, u32[]{:S(2)}) copy-start(bf16[16,128,128]{2,1,0:T(8,128)(2,1)} %get-tuple-element.18) | copy-start | bytes 1572868
  13.1 14.9 %copy-start.6 = (s32[4]{0:T(128)S(1)}, s32[4]{0:T(128)}, u32[]{:S(2)}) copy-start(s32[4]{0:T(128)} %pad_add_fusion.where_ref) | copy-start | bytes 52
  13.1 14.9 %copy-start.7 = (s32[512]{0:T(512)S(1)}, s32[512]{0:T(512)}, u32[]{:S(2)}) copy-start(s32[512]{0:T(512)} %param.11) | copy-start | bytes 6148
  13.1 14.9 %copy-start.8 = (s32[256]{0:T(256)S(1)}, s32[256]{0:T(256)}, u32[]{:S(2)}) copy-start(s32[256]{0:T(256)} %param.10) | copy-start | bytes 3076
  13.1 29.1 %all-to-all-start = ((bf16[16,384,128]{2,1,0:T(8,128)(2,1)}), bf16[16,384,128]{2,1,0:T(8,128)(2,1)S(1)}, u32[]{:S(2)}, u32[]{:S(2)}) async-start(bf16[16,384,128]{2,1,0:T(8,128)(2,1)} %get-tuple-element.16), calls=%async_computation | async-start | bytes 3145728 | tf_op jit(solution)/shard_map/all_to_all | solution.py:357
  20.7 39.2 %collective-permute-start = (bf16[16,128,128]{2,1,0:T(8,128)(2,1)S(1)}, bf16[16,128,128]{2,1,0:T(8,128)(2,1)S(1)}, u32[]{:S(2)}, u32[]{:S(2)}) collective-permute-start(bf16[16,128,128]{2,1,0:T(8,128)(2,1)S(1)} %copy-done.9), channel_id=1, source_target_pairs={{0,4},{4,0},{1,5},{5,1},{2,6},{6,2},{3,7},{7,3},{8,12},{12,8},{9,1... | collective-permute-start | bytes 1572872 | tf_op jit(solution)/shard_map/ppermute | solution.py:320
  28.0 3.4 %copy-start = (bf16[16,2,512,256]{3,2,1,0:T(8,128)(2,1)S(1)}, bf16[16,2,512,256]{3,2,1,0:T(8,128)(2,1)}, u32[]{:S(2)}) copy-start(bf16[16,2,512,256]{3,2,1,0:T(8,128)(2,1)} %weights_ref.1) | copy-start | bytes 25165828
  38.4 2.0 %copy-start.2 = (bf16[8,512,512]{2,1,0:T(8,128)(2,1)}, bf16[8,512,512]{2,1,0:T(8,128)(2,1)S(1)}, u32[]{:S(2)}) copy-start(bf16[8,512,512]{2,1,0:T(8,128)(2,1)S(1)} %shard_map.83.weights_ref) | copy-start | bytes 12582916
  42.3 37.0 %collective-permute-start.7 = (bf16[16,8,16,128]{3,2,1,0:T(8,128)(2,1)S(1)}, bf16[16,8,16,128]{3,2,1,0:T(8,128)(2,1)S(1)}, u32[]{:S(2)}, u32[]{:S(2)}) collective-permute-start(bf16[16,8,16,128]{3,2,1,0:T(8,128)(2,1)S(1)} %slice.142), channel_id=1, source_target_pairs={{0,4},{4,0},{1,5},{5,1},{2,6},{6,2},{3,7},{7,3},{8,12},{12,8},{9,1... | collective-permute-start | bytes 1572872 | tf_op jit(solution)/shard_map/ppermute | solution.py:320
  49.5 3.4 %copy-start.1 = (bf16[16,2,512,256]{3,2,1,0:T(8,128)(2,1)S(1)}, bf16[16,2,512,256]{3,2,1,0:T(8,128)(2,1)}, u32[]{:S(2)}) copy-start(bf16[16,2,512,256]{3,2,1,0:T(8,128)(2,1)} %weights_ref.1) | copy-start | bytes 25165828
  52.9 26.3 %copy-start.3 = (bf16[8,512,512]{2,1,0:T(8,128)(2,1)S(1)}, bf16[8,512,512]{2,1,0:T(8,128)(2,1)}, u32[]{:S(2)}) copy-start(bf16[8,512,512]{2,1,0:T(8,128)(2,1)} %copy-done.2) | copy-start | bytes 12582916
  59.9 5.7 %collective-permute-start.1 = (bf16[4,128,128]{2,1,0:T(8,128)(2,1)S(1)}, bf16[4,128,128]{2,1,0:T(8,128)(2,1)S(1)}, u32[]{:S(2)}, u32[]{:S(2)}) collective-permute-start(bf16[4,128,128]{2,1,0:T(8,128)(2,1)S(1)} %get-tuple-element.31), channel_id=1, source_target_pairs={{0,8},{8,0},{16,24},{24,16},{1,9},{9,1},{17,25},{25,17},{2,10},{10... | collective-permute-start | bytes 393224 | tf_op jit(solution)/shard_map/ppermute | solution.py:320
  60.0 8.8 %collective-permute-start.3 = (bf16[4,128,128]{2,1,0:T(8,128)(2,1)S(1)}, bf16[4,128,128]{2,1,0:T(8,128)(2,1)S(1)}, u32[]{:S(2)}, u32[]{:S(2)}) collective-permute-start(bf16[4,128,128]{2,1,0:T(8,128)(2,1)S(1)} %get-tuple-element.32), channel_id=1, source_target_pairs={{0,24},{8,16},{16,8},{24,0},{1,25},{9,17},{17,9},{25,1},{2,26},{10... | collective-permute-start | bytes 393224 | tf_op jit(solution)/shard_map/ppermute | solution.py:320
  61.4 7.4 %collective-permute-start.2 = (bf16[4,128,128]{2,1,0:T(8,128)(2,1)S(1)}, bf16[4,128,128]{2,1,0:T(8,128)(2,1)S(1)}, u32[]{:S(2)}, u32[]{:S(2)}) collective-permute-start(bf16[4,128,128]{2,1,0:T(8,128)(2,1)S(1)} %get-tuple-element.33), channel_id=1, source_target_pairs={{0,16},{8,24},{16,0},{24,8},{1,17},{9,25},{17,1},{25,9},{2,18},{10... | collective-permute-start | bytes 393224 | tf_op jit(solution)/shard_map/ppermute | solution.py:320
  68.9 6.0 %collective-permute-start.4 = (bf16[4,128,128]{2,1,0:T(8,128)(2,1)S(1)}, bf16[4,128,128]{2,1,0:T(8,128)(2,1)S(1)}, u32[]{:S(2)}, u32[]{:S(2)}) collective-permute-start(bf16[4,128,128]{2,1,0:T(8,128)(2,1)S(1)} %pad_maximum_fusion.1), channel_id=1, source_target_pairs={{0,1},{1,0},{2,3},{3,2},{4,5},{5,4},{6,7},{7,6},{8,9},{9,8},{10,11... | collective-permute-start | bytes 393224 | tf_op jit(solution)/shard_map/ppermute | solution.py:320
  71.2 6.7 %collective-permute-start.5 = (bf16[4,128,128]{2,1,0:T(8,128)(2,1)S(1)}, bf16[4,128,128]{2,1,0:T(8,128)(2,1)S(1)}, u32[]{:S(2)}, u32[]{:S(2)}) collective-permute-start(bf16[4,128,128]{2,1,0:T(8,128)(2,1)S(1)} %pad_maximum_fusion.2), channel_id=1, source_target_pairs={{0,2},{1,3},{2,0},{3,1},{4,6},{5,7},{6,4},{7,5},{8,10},{9,11},{10,... | collective-permute-start | bytes 393224 | tf_op jit(solution)/shard_map/ppermute | solution.py:320
  73.0 6.2 %collective-permute-start.6 = (bf16[4,128,128]{2,1,0:T(8,128)(2,1)S(1)}, bf16[4,128,128]{2,1,0:T(8,128)(2,1)S(1)}, u32[]{:S(2)}, u32[]{:S(2)}) collective-permute-start(bf16[4,128,128]{2,1,0:T(8,128)(2,1)S(1)} %pad_maximum_fusion.3), channel_id=1, source_target_pairs={{0,3},{1,2},{2,1},{3,0},{4,7},{5,6},{6,5},{7,4},{8,11},{9,10},{10,... | collective-permute-start | bytes 393224 | tf_op jit(solution)/shard_map/ppermute | solution.py:320
  82.1 3.5 %collective-permute-start.8 = (bf16[2,2,8,2,64,128]{5,4,3,2,1,0:T(8,128)(2,1)S(1)}, bf16[2,2,8,2,64,128]{5,4,3,2,1,0:T(8,128)(2,1)S(1)}, u32[]{:S(2)}, u32[]{:S(2)}) collective-permute-start(bf16[2,2,8,2,64,128]{5,4,3,2,1,0:T(8,128)(2,1)S(1)} %get-tuple-element.24), channel_id=1, source_target_pairs={{0,32},{32,0},{1,33},{33,1},{2,34},{34,2},{3,35},{35,3},{4,36},{36... | collective-permute-start | bytes 3145736 | tf_op jit(solution)/shard_map/ppermute | solution.py:320
  84.9 2.9 %collective-permute-start.11 = (bf16[2,2,8,2,64,128]{5,4,3,2,1,0:T(8,128)(2,1)S(1)}, bf16[2,2,8,2,64,128]{5,4,3,2,1,0:T(8,128)(2,1)S(1)}, u32[]{:S(2)}, u32[]{:S(2)}) collective-permute-start(bf16[2,2,8,2,64,128]{5,4,3,2,1,0:T(8,128)(2,1)S(1)} %get-tuple-element.26), channel_id=1, source_target_pairs={{0,32},{32,0},{1,33},{33,1},{2,34},{34,2},{3,35},{35,3},{4,36},{36... | collective-permute-start | bytes 3145736 | tf_op jit(solution)/shard_map/ppermute | solution.py:320
  85.7 26.2 %collective-permute-start.9 = (bf16[2,8,2,64,128]{4,3,2,1,0:T(8,128)(2,1)S(1)}, bf16[2,8,2,64,128]{4,3,2,1,0:T(8,128)(2,1)S(1)}, u32[]{:S(2)}, u32[]{:S(2)}) collective-permute-start(bf16[2,8,2,64,128]{4,3,2,1,0:T(8,128)(2,1)S(1)} %fusion), channel_id=1, source_target_pairs={{0,128},{64,192},{128,0},{192,64},{1,129},{65,193},{129,1},{193,65... | collective-permute-start | bytes 1572872 | tf_op jit(solution)/shard_map/ppermute | solution.py:320
  87.8 39.7 %copy-start.4 = (bf16[2,256,256]{2,1,0:T(8,128)(2,1)S(1)}, bf16[2,256,256]{2,1,0:T(8,128)(2,1)}, u32[]{:S(2)}) copy-start(bf16[2,256,256]{2,1,0:T(8,128)(2,1)} %constant.32.clone.refs_8_) | copy-start | bytes 786436
  87.8 39.7 %copy-start.5 = (f32[16,128]{1,0:T(8,128)S(1)}, f32[16,128]{1,0:T(8,128)}, u32[]{:S(2)}) copy-start(f32[16,128]{1,0:T(8,128)} %constant.33.clone.refs_9_) | copy-start | bytes 24580
  88.0 25.0 %collective-permute-start.12 = (bf16[2,8,2,64,128]{4,3,2,1,0:T(8,128)(2,1)S(1)}, bf16[2,8,2,64,128]{4,3,2,1,0:T(8,128)(2,1)S(1)}, u32[]{:S(2)}, u32[]{:S(2)}) collective-permute-start(bf16[2,8,2,64,128]{4,3,2,1,0:T(8,128)(2,1)S(1)} %fusion.1), channel_id=1, source_target_pairs={{0,64},{64,0},{128,192},{192,128},{1,65},{65,1},{129,193},{193,129... | collective-permute-start | bytes 1572872 | tf_op jit(solution)/shard_map/ppermute | solution.py:320
  112.0 11.7 %collective-permute-start.10 = (bf16[8,2,64,128]{3,2,1,0:T(8,128)(2,1)S(1)}, bf16[8,2,64,128]{3,2,1,0:T(8,128)(2,1)S(1)}, u32[]{:S(2)}, u32[]{:S(2)}) collective-permute-start(bf16[8,2,64,128]{3,2,1,0:T(8,128)(2,1)S(1)} %fusion.3), channel_id=1, source_target_pairs={{0,64},{64,0},{128,192},{192,128},{1,65},{65,1},{129,193},{193,129... | collective-permute-start | bytes 786440 | tf_op jit(solution)/shard_map/ppermute | solution.py:320
  113.1 14.4 %collective-permute-start.13 = (bf16[8,2,64,128]{3,2,1,0:T(8,128)(2,1)S(1)}, bf16[8,2,64,128]{3,2,1,0:T(8,128)(2,1)S(1)}, u32[]{:S(2)}, u32[]{:S(2)}) collective-permute-start(bf16[8,2,64,128]{3,2,1,0:T(8,128)(2,1)S(1)} %fusion.2), channel_id=1, source_target_pairs={{0,128},{64,192},{128,0},{192,64},{1,129},{65,193},{129,1},{193,65... | collective-permute-start | bytes 786440 | tf_op jit(solution)/shard_map/ppermute | solution.py:320

commit v3 on v2

--- a/solution.py
+++ b/solution.py
@@ -187,9 +187,13 @@
         place_ref[0:feeds] = jnp.where(is_imag == 0, match, jnp.zeros_like(match))
         place_ref[feeds:] = jnp.where(is_imag == 1, match, jnp.zeros_like(match))
 
-    wide = jnp.concatenate([weights_ref[0, 0], weights_ref[0, 1]], axis=1)
-    picked = product(pick_ref[...], wide, 0)
-    out_ref[0] = product(picked, place_ref[...], 0)
+    for chan in range(weights_ref.shape[0]):
+        wide = jnp.concatenate([weights_ref[chan, 0], weights_ref[chan, 1]], axis=1)
+        picked = product(pick_ref[...], wide, 0)
+        out_ref[chan] = product(picked, place_ref[...], 0)
+
+
+PER_STEP = 2
 
 
 def arrange_weights(where, weights, order, inputs_map, chunk):
@@ -199,20 +203,20 @@
         functools.partial(weight_kernel, chunk == 0),
         grid_spec=pltpu.PrefetchScalarGridSpec(
             num_scalar_prefetch=1,
-            grid=(chans,),
+            grid=(chans // PER_STEP,),
             in_specs=[
                 pl.BlockSpec((1, beams), lambda c, w: (0, 0)),
                 pl.BlockSpec((1, feeds), lambda c, w: (0, 0)),
-                pl.BlockSpec((1, 2, beams, feeds), lambda c, w: (chunk * chans + c, 0, 0, 0)),
+                pl.BlockSpec((PER_STEP, 2, beams, feeds), lambda c, w: (chunk * chans // PER_STEP + c, 0, 0, 0)),
             ],
-            out_specs=pl.BlockSpec((1, beams, 2 * feeds), lambda c, w: (c, 0, 0)),
+            out_specs=pl.BlockSpec((PER_STEP, beams, 2 * feeds), lambda c, w: (c, 0, 0)),
             scratch_shapes=[
                 pltpu.VMEM((beams, beams), jnp.bfloat16),
                 pltpu.VMEM((2 * feeds, 2 * feeds), jnp.bfloat16),
             ],
         ),
         out_shape=jax.ShapeDtypeStruct((chans, beams, 2 * feeds), jnp.bfloat16),
-        compiler_params=pltpu.CompilerParams(vmem_limit_bytes=SMALL),
+        compiler_params=pltpu.CompilerParams(vmem_limit_bytes=LARGE),
         cost_estimate=SHORT,
     )(where, order.reshape(1, beams), inputs_map.reshape(1, feeds), weights)
 
@@ -362,8 +366,8 @@
     planed = turn(rest)
     far1 = swap(planed[:, :half], "zh", 1, 2)
     arranged0 = arrange_weights(where, after(weights, rest), beam_order, input_map, 0)
-    arranged1 = arrange_weights(where, after(after(weights, planed), arranged0), beam_order, input_map, 1)
-    data0 = after(turn_by_swaps(after(far0, arranged1)), far1)
+    arranged1 = arrange_weights(where, after(weights, arranged0), beam_order, input_map, 1)
+    data0 = after(turn_by_swaps(after(after(far0, arranged1), planed)), far1)
 
     keep0, send0 = combine(arranged0, planed, half, data0, 0)
     come0 = swap(send0, "core", 1, 2)

time: 130 us -> 127 us (0.977)
  local copies, waits for them, and re-layouts: 8.85 us -> 0.13 us
  starting transfers between devices: 35.8 us -> 42.5 us
  waiting for transfers between devices: 49.4 us -> 43.9 us
  Pallas kernels: 34.1 us -> 38.3 us
    unnamed x20 -> x10, local copies, waits for them, and re-layouts: 8.74 us -> 0.02 us
    ppermute x14, starting transfers between devices: 28.2 us -> 34.9 us  [swap(): return lax.ppermute(value, axis, [(k, k ^ distance) for k in range(size)])]
    pallas_call x2, Pallas kernels: 13.9 us -> 18.1 us  [arrange_weights(): pl.pallas_call(functools.partial(weight_kernel, chunk == 0), grid_spec=pl...]
    ppermute x14, waiting for transfers between devices: 47.5 us -> 43.9 us  [swap(): return lax.ppermute(value, axis, [(k, k ^ distance) for k in range(size)])]
    all_to_all x1, waiting for transfers between devices: 1.9 us -> 0.01 us  [turn(): lax.all_to_all(value.reshape(PLANE, -1, SPECTRA), ('y', 'x'), split_axis=...]
  transfers between devices with their start and end apart: 15 -> 15, of which waited for: 11 -> 10; matrix products, arithmetic and copies ran while one was open for 1% -> 1% of each run, Pallas kernels for 13% -> 17%
where the time goes in v3:
time: 127 us; the launch traced here: 126 us
  waiting for transfers between devices  43.9 us (35%)
  starting transfers between devices  42.5 us (33%)
  Pallas kernels  38.3 us (30%)
    ppermute x14, waiting for transfers between devices, swap(): return lax.ppermute(value, axis, [(k, k ^ distance) for k in range(size)])  43.9 us
    ppermute x14, starting transfers between devices, swap(): return lax.ppermute(value, axis, [(k, k ^ distance) for k in range(size)])  34.9 us
    pallas_call x2, Pallas kernels, arrange_weights(): pl.pallas_call(functools.partial(weight_kernel, chunk == 0), grid_spec=pl...  18.1 us
    pallas_call x1, Pallas kernels, channelize(): pl.pallas_call(channelize_kernel, out_shape=(first, rest), in_specs=[pl.B...  12.4 us
    all_to_all x1, starting transfers between devices, turn(): lax.all_to_all(value.reshape(PLANE, -1, SPECTRA), ('y', 'x'), split_axis=...  7.62 us
    pallas_call x2, Pallas kernels, combine(): pl.pallas_call(functools.partial(combine_kernel, chunk == 1), grid=(chans...  5.6 us
  transfers between devices with their start and end apart: 15, of which 10 were waited for; matrix products, arithmetic and copies ran while one was open for 1% of the time, Pallas kernels for 17%

profile of v3, /device:TPU:2, one launch (start us, length us, event | category | flops | bytes accessed | tf_op | source)
XLA Modules:
  0.0 126.2 jit_solution(7778444728871091033)
XLA Ops:
  0.0 0.6 pad_add_fusion.where_ref
  0.6 12.4 %shard_map.82 = (bf16[16,128,128]{2,1,0:T(8,128)(2,1)}, bf16[16,384,128]{2,1,0:T(8,128)(2,1)}) custom-call(s32[4]{0:T(128)} %pad_add_fusion.where_ref, bf16[8,268288]{1,0:T(8,128)(2,1)} %volts_hbm.1, f32[4,8,2048]{2,1,0:T(8,128)} %constant.31.clone.taper_ref, bf16[2,2,256,2048]{3,2,1,0:T(8,128)(2,1)} %constant.30.clone.table_hbm), custom_call_target="tpu_custom_call" | custom-call | flops 1 | bytes 1 | tf_op jit(solution)/shard_map/pallas_call | solution.py:133
  13.0 0.0 copy-start.4
  13.1 7.6 %all-to-all-start = ((bf16[16,384,128]{2,1,0:T(8,128)(2,1)}), bf16[16,384,128]{2,1,0:T(8,128)(2,1)S(1)}, u32[]{:S(2)}, u32[]{:S(2)}) async-start(bf16[16,384,128]{2,1,0:T(8,128)(2,1)} %get-tuple-element.16), calls=%async_computation | async-start | bytes 3145728 | tf_op jit(solution)/shard_map/all_to_all | solution.py:361
  20.7 0.0 copy-done.4
  20.7 7.3 %collective-permute-start = (bf16[16,128,128]{2,1,0:T(8,128)(2,1)S(1)}, bf16[16,128,128]{2,1,0:T(8,128)(2,1)S(1)}, u32[]{:S(2)}, u32[]{:S(2)}) collective-permute-start(bf16[16,128,128]{2,1,0:T(8,128)(2,1)S(1)} %copy-done.4), channel_id=1, source_target_pairs={{0,4},{4,0},{1,5},{5,1},{2,6},{6,2},{3,7},{7,3},{8,12},{12,8},{9,1... | collective-permute-start | bytes 1572872 | tf_op jit(solution)/shard_map/ppermute | solution.py:324
  28.0 9.0 %shard_map.83.weights_ref = bf16[8,512,512]{2,1,0:T(8,128)(2,1)} custom-call(s32[4]{0:T(128)} %pad_add_fusion.where_ref, s32[1,512]{1,0:T(1,128)} %bitcast.38, s32[1,256]{1,0:T(1,128)} %bitcast.40, bf16[16,2,512,256]{3,2,1,0:T(8,128)(2,1)} %weights_ref.1), custom_call_target="tpu_custom_call" | custom-call | flops 1 | bytes 1 | tf_op jit(solution)/shard_map/pallas_call | solution.py:202
  36.9 9.1 %shard_map.84.weights_ref = bf16[8,512,512]{2,1,0:T(8,128)(2,1)} custom-call(s32[4]{0:T(128)} %pad_add_fusion.where_ref, s32[1,512]{1,0:T(1,128)} %bitcast.39, s32[1,256]{1,0:T(1,128)} %bitcast.41, bf16[16,2,512,256]{3,2,1,0:T(8,128)(2,1)} %weights_ref.1), custom_call_target="tpu_custom_call" | custom-call | flops 1 | bytes 1 | tf_op jit(solution)/shard_map/pallas_call | solution.py:202
  46.0 0.0 collective-permute-done
  46.0 0.0 all-to-all-done
  46.0 0.0 copy-start.1
  46.1 9.7 %collective-permute-start.7 = (bf16[16,8,16,128]{3,2,1,0:T(8,128)(2,1)S(1)}, bf16[16,8,16,128]{3,2,1,0:T(8,128)(2,1)S(1)}, u32[]{:S(2)}, u32[]{:S(2)}) collective-permute-start(bf16[16,8,16,128]{3,2,1,0:T(8,128)(2,1)S(1)} %slice.142), channel_id=1, source_target_pairs={{0,4},{4,0},{1,5},{5,1},{2,6},{6,2},{3,7},{7,3},{8,12},{12,8},{9,1... | collective-permute-start | bytes 1572872 | tf_op jit(solution)/shard_map/ppermute | solution.py:324
  55.9 1.6 %collective-permute-start.1 = (bf16[4,128,128]{2,1,0:T(8,128)(2,1)S(1)}, bf16[4,128,128]{2,1,0:T(8,128)(2,1)S(1)}, u32[]{:S(2)}, u32[]{:S(2)}) collective-permute-start(bf16[4,128,128]{2,1,0:T(8,128)(2,1)S(1)} %get-tuple-element.31), channel_id=1, source_target_pairs={{0,8},{8,0},{16,24},{24,16},{1,9},{9,1},{17,25},{25,17},{2,10},{10... | collective-permute-start | bytes 393224 | tf_op jit(solution)/shard_map/ppermute | solution.py:324
  57.4 2.1 %collective-permute-start.3 = (bf16[4,128,128]{2,1,0:T(8,128)(2,1)S(1)}, bf16[4,128,128]{2,1,0:T(8,128)(2,1)S(1)}, u32[]{:S(2)}, u32[]{:S(2)}) collective-permute-start(bf16[4,128,128]{2,1,0:T(8,128)(2,1)S(1)} %get-tuple-element.32), channel_id=1, source_target_pairs={{0,24},{8,16},{16,8},{24,0},{1,25},{9,17},{17,9},{25,1},{2,26},{10... | collective-permute-start | bytes 393224 | tf_op jit(solution)/shard_map/ppermute | solution.py:324
  59.5 0.6 collective-permute-start.2
  60.1 0.8 collective-permute-done.1
  60.9 2.7 %collective-permute-done.3 = bf16[4,128,128]{2,1,0:T(8,128)(2,1)S(1)} collective-permute-done((bf16[4,128,128]{2,1,0:T(8,128)(2,1)S(1)}, bf16[4,128,128]{2,1,0:T(8,128)(2,1)S(1)}, u32[]{:S(2)}, u32[]{:S(2)}) %collective-permute-start.3) | collective-permute-done | bytes 131104 | tf_op jit(solution)/shard_map/ppermute | solution.py:324
  63.6 2.4 %collective-permute-done.2 = bf16[4,128,128]{2,1,0:T(8,128)(2,1)S(1)} collective-permute-done((bf16[4,128,128]{2,1,0:T(8,128)(2,1)S(1)}, bf16[4,128,128]{2,1,0:T(8,128)(2,1)S(1)}, u32[]{:S(2)}, u32[]{:S(2)}) %collective-permute-start.2) | collective-permute-done | bytes 131104 | tf_op jit(solution)/shard_map/ppermute | solution.py:324
  66.0 0.6 collective-permute-start.4
  66.7 2.6 %collective-permute-start.5 = (bf16[4,128,128]{2,1,0:T(8,128)(2,1)S(1)}, bf16[4,128,128]{2,1,0:T(8,128)(2,1)S(1)}, u32[]{:S(2)}, u32[]{:S(2)}) collective-permute-start(bf16[4,128,128]{2,1,0:T(8,128)(2,1)S(1)} %pad_maximum_fusion.2), channel_id=1, source_target_pairs={{0,2},{1,3},{2,0},{3,1},{4,6},{5,7},{6,4},{7,5},{8,10},{9,11},{10,... | collective-permute-start | bytes 393224 | tf_op jit(solution)/shard_map/ppermute | solution.py:324
  69.3 0.7 collective-permute-start.6
  70.0 1.1 collective-permute-done.4
  71.1 2.4 %collective-permute-done.5 = bf16[4,128,128]{2,1,0:T(8,128)(2,1)S(1)} collective-permute-done((bf16[4,128,128]{2,1,0:T(8,128)(2,1)S(1)}, bf16[4,128,128]{2,1,0:T(8,128)(2,1)S(1)}, u32[]{:S(2)}, u32[]{:S(2)}) %collective-permute-start.5) | collective-permute-done | bytes 131104 | tf_op jit(solution)/shard_map/ppermute | solution.py:324
  73.5 1.4 %collective-permute-done.6 = bf16[4,128,128]{2,1,0:T(8,128)(2,1)S(1)} collective-permute-done((bf16[4,128,128]{2,1,0:T(8,128)(2,1)S(1)}, bf16[4,128,128]{2,1,0:T(8,128)(2,1)S(1)}, u32[]{:S(2)}, u32[]{:S(2)}) %collective-permute-start.6) | collective-permute-done | bytes 131104 | tf_op jit(solution)/shard_map/ppermute | solution.py:324
  74.8 0.1 pad_maximum_fusion
  74.9 0.0 collective-permute-done.7.far_ref
  74.9 0.0 copy-done.1
  74.9 0.0 copy-start
  74.9 2.8 %shard_map.85 = (f32[2,2,8,2,64,128]{5,4,3,2,1,0:T(8,128)S(1)}, bf16[2,2,8,2,64,128]{5,4,3,2,1,0:T(8,128)(2,1)S(1)}) custom-call(bf16[8,512,512]{2,1,0:T(8,128)(2,1)S(1)} %copy-done.1, bf16[16,24,16,128]{3,2,1,0:T(8,128)(2,1)S(1)} %bitcast.32, bf16[16,8,16,128]{3,2,1,0:T(8,128)(2,1)S(1)} %bitcast.34), custom_call_target="tpu_custom_call" | custom-call | flops 1 | bytes 1 | tf_op jit(solution)/shard_map/pallas_call | solution.py:249
  77.7 0.1 collective-permute-start.8
  77.8 0.0 copy-done
  77.8 2.8 %shard_map.86 = (f32[2,2,8,2,64,128]{5,4,3,2,1,0:T(8,128)S(1)}, bf16[2,2,8,2,64,128]{5,4,3,2,1,0:T(8,128)(2,1)S(1)}) custom-call(bf16[8,512,512]{2,1,0:T(8,128)(2,1)S(1)} %copy-done, bf16[16,24,16,128]{3,2,1,0:T(8,128)(2,1)S(1)} %bitcast.33, bf16[16,8,16,128]{3,2,1,0:T(8,128)(2,1)S(1)} %collective-permute-done.7.far_ref), custom_call_target="tpu_custom_call" | custom-call | flops 1 | bytes 1 | tf_op jit(solution)/shard_map/pallas_call | solution.py:249
  80.6 0.6 collective-permute-start.11
  81.2 0.0 collective-permute-done.8.refs_1_
  81.2 0.2 fusion
  81.4 4.6 %collective-permute-start.9 = (bf16[2,8,2,64,128]{4,3,2,1,0:T(8,128)(2,1)S(1)}, bf16[2,8,2,64,128]{4,3,2,1,0:T(8,128)(2,1)S(1)}, u32[]{:S(2)}, u32[]{:S(2)}) collective-permute-start(bf16[2,8,2,64,128]{4,3,2,1,0:T(8,128)(2,1)S(1)} %fusion), channel_id=1, source_target_pairs={{0,128},{64,192},{128,0},{192,64},{1,129},{65,193},{129,1},{193,65... | collective-permute-start | bytes 1572872 | tf_op jit(solution)/shard_map/ppermute | solution.py:324
  85.9 0.0 collective-permute-done.11.refs_5_
  85.9 0.0 copy-start.2
  85.9 0.0 copy-start.3
  85.9 0.2 fusion.1
  86.1 1.9 %collective-permute-start.12 = (bf16[2,8,2,64,128]{4,3,2,1,0:T(8,128)(2,1)S(1)}, bf16[2,8,2,64,128]{4,3,2,1,0:T(8,128)(2,1)S(1)}, u32[]{:S(2)}, u32[]{:S(2)}) collective-permute-start(bf16[2,8,2,64,128]{4,3,2,1,0:T(8,128)(2,1)S(1)} %fusion.1), channel_id=1, source_target_pairs={{0,64},{64,0},{128,192},{192,128},{1,65},{65,1},{129,193},{193,129... | collective-permute-start | bytes 1572872 | tf_op jit(solution)/shard_map/ppermute | solution.py:324
  88.0 21.4 %collective-permute-done.9.refs_2_ = bf16[2,8,2,64,128]{4,3,2,1,0:T(8,128)(2,1)S(1)} collective-permute-done((bf16[2,8,2,64,128]{4,3,2,1,0:T(8,128)(2,1)S(1)}, bf16[2,8,2,64,128]{4,3,2,1,0:T(8,128)(2,1)S(1)}, u32[]{:S(2)}, u32[]{:S(2)}) %collective-permute-start.9) | collective-permute-done | bytes 524320 | tf_op jit(solution)/shard_map/ppermute | solution.py:324
  109.4 0.1 fusion.3
  109.5 0.1 collective-permute-start.10
  109.6 0.1 collective-permute-done.12.refs_6_
  109.8 0.1 fusion.2
  109.9 2.6 %collective-permute-start.13 = (bf16[8,2,64,128]{3,2,1,0:T(8,128)(2,1)S(1)}, bf16[8,2,64,128]{3,2,1,0:T(8,128)(2,1)S(1)}, u32[]{:S(2)}, u32[]{:S(2)}) collective-permute-start(bf16[8,2,64,128]{3,2,1,0:T(8,128)(2,1)S(1)} %fusion.2), channel_id=1, source_target_pairs={{0,128},{64,192},{128,0},{192,64},{1,129},{65,193},{129,1},{193,65... | collective-permute-start | bytes 786440 | tf_op jit(solution)/shard_map/ppermute | solution.py:324
  112.4 9.7 %collective-permute-done.10.refs_3_ = bf16[8,2,64,128]{3,2,1,0:T(8,128)(2,1)S(1)} collective-permute-done((bf16[8,2,64,128]{3,2,1,0:T(8,128)(2,1)S(1)}, bf16[8,2,64,128]{3,2,1,0:T(8,128)(2,1)S(1)}, u32[]{:S(2)}, u32[]{:S(2)}) %collective-permute-start.10) | collective-permute-done | bytes 262176 | tf_op jit(solution)/shard_map/ppermute | solution.py:324
  122.2 1.9 %collective-permute-done.13.refs_7_ = bf16[8,2,64,128]{3,2,1,0:T(8,128)(2,1)S(1)} collective-permute-done((bf16[8,2,64,128]{3,2,1,0:T(8,128)(2,1)S(1)}, bf16[8,2,64,128]{3,2,1,0:T(8,128)(2,1)S(1)}, u32[]{:S(2)}, u32[]{:S(2)}) %collective-permute-start.13) | collective-permute-done | bytes 262176 | tf_op jit(solution)/shard_map/ppermute | solution.py:324
  124.1 0.0 copy-done.2
  124.1 0.0 copy-done.3
  124.1 2.1 %shard_map.87 = f32[16,16,64]{2,1,0:T(8,128)} custom-call(f32[2,2,8,2,64,128]{5,4,3,2,1,0:T(8,128)S(1)} %get-tuple-element.23.refs_0_, bf16[2,2,8,2,64,128]{5,4,3,2,1,0:T(8,128)(2,1)S(1)} %collective-permute-done.8.refs_1_, bf16[2,8,2,64,128]{4,3,2,1,0:T(8,128)(2,1)S(1)} %collective-permute-done.9.refs_2_, ...), custom_call_target="tpu_custom_call" | custom-call | flops 1 | bytes 1 | tf_op jit(solution)/shard_map/pallas_call | solution.py:312
  (10 shorter events, 0.2 us)
Async XLA Ops:
  13.0 7.6 %copy-start.4 = (bf16[16,128,128]{2,1,0:T(8,128)(2,1)S(1)}, bf16[16,128,128]{2,1,0:T(8,128)(2,1)}, u32[]{:S(2)}) copy-start(bf16[16,128,128]{2,1,0:T(8,128)(2,1)} %get-tuple-element.18) | copy-start | bytes 1572868
  13.1 33.0 %all-to-all-start = ((bf16[16,384,128]{2,1,0:T(8,128)(2,1)}), bf16[16,384,128]{2,1,0:T(8,128)(2,1)S(1)}, u32[]{:S(2)}, u32[]{:S(2)}) async-start(bf16[16,384,128]{2,1,0:T(8,128)(2,1)} %get-tuple-element.16), calls=%async_computation | async-start | bytes 3145728 | tf_op jit(solution)/shard_map/all_to_all | solution.py:361
  20.7 25.4 %collective-permute-start = (bf16[16,128,128]{2,1,0:T(8,128)(2,1)S(1)}, bf16[16,128,128]{2,1,0:T(8,128)(2,1)S(1)}, u32[]{:S(2)}, u32[]{:S(2)}) collective-permute-start(bf16[16,128,128]{2,1,0:T(8,128)(2,1)S(1)} %copy-done.4), channel_id=1, source_target_pairs={{0,4},{4,0},{1,5},{5,1},{2,6},{6,2},{3,7},{7,3},{8,12},{12,8},{9,1... | collective-permute-start | bytes 1572872 | tf_op jit(solution)/shard_map/ppermute | solution.py:324
  46.0 28.9 %copy-start.1 = (bf16[8,512,512]{2,1,0:T(8,128)(2,1)S(1)}, bf16[8,512,512]{2,1,0:T(8,128)(2,1)}, u32[]{:S(2)}) copy-start(bf16[8,512,512]{2,1,0:T(8,128)(2,1)} %shard_map.83.weights_ref) | copy-start | bytes 12582916
  46.1 28.8 %collective-permute-start.7 = (bf16[16,8,16,128]{3,2,1,0:T(8,128)(2,1)S(1)}, bf16[16,8,16,128]{3,2,1,0:T(8,128)(2,1)S(1)}, u32[]{:S(2)}, u32[]{:S(2)}) collective-permute-start(bf16[16,8,16,128]{3,2,1,0:T(8,128)(2,1)S(1)} %slice.142), channel_id=1, source_target_pairs={{0,4},{4,0},{1,5},{5,1},{2,6},{6,2},{3,7},{7,3},{8,12},{12,8},{9,1... | collective-permute-start | bytes 1572872 | tf_op jit(solution)/shard_map/ppermute | solution.py:324
  55.9 5.1 %collective-permute-start.1 = (bf16[4,128,128]{2,1,0:T(8,128)(2,1)S(1)}, bf16[4,128,128]{2,1,0:T(8,128)(2,1)S(1)}, u32[]{:S(2)}, u32[]{:S(2)}) collective-permute-start(bf16[4,128,128]{2,1,0:T(8,128)(2,1)S(1)} %get-tuple-element.31), channel_id=1, source_target_pairs={{0,8},{8,0},{16,24},{24,16},{1,9},{9,1},{17,25},{25,17},{2,10},{10... | collective-permute-start | bytes 393224 | tf_op jit(solution)/shard_map/ppermute | solution.py:324
  57.4 6.2 %collective-permute-start.3 = (bf16[4,128,128]{2,1,0:T(8,128)(2,1)S(1)}, bf16[4,128,128]{2,1,0:T(8,128)(2,1)S(1)}, u32[]{:S(2)}, u32[]{:S(2)}) collective-permute-start(bf16[4,128,128]{2,1,0:T(8,128)(2,1)S(1)} %get-tuple-element.32), channel_id=1, source_target_pairs={{0,24},{8,16},{16,8},{24,0},{1,25},{9,17},{17,9},{25,1},{2,26},{10... | collective-permute-start | bytes 393224 | tf_op jit(solution)/shard_map/ppermute | solution.py:324
  59.5 6.5 %collective-permute-start.2 = (bf16[4,128,128]{2,1,0:T(8,128)(2,1)S(1)}, bf16[4,128,128]{2,1,0:T(8,128)(2,1)S(1)}, u32[]{:S(2)}, u32[]{:S(2)}) collective-permute-start(bf16[4,128,128]{2,1,0:T(8,128)(2,1)S(1)} %get-tuple-element.33), channel_id=1, source_target_pairs={{0,16},{8,24},{16,0},{24,8},{1,17},{9,25},{17,1},{25,9},{2,18},{10... | collective-permute-start | bytes 393224 | tf_op jit(solution)/shard_map/ppermute | solution.py:324
  66.0 5.1 %collective-permute-start.4 = (bf16[4,128,128]{2,1,0:T(8,128)(2,1)S(1)}, bf16[4,128,128]{2,1,0:T(8,128)(2,1)S(1)}, u32[]{:S(2)}, u32[]{:S(2)}) collective-permute-start(bf16[4,128,128]{2,1,0:T(8,128)(2,1)S(1)} %pad_maximum_fusion.1), channel_id=1, source_target_pairs={{0,1},{1,0},{2,3},{3,2},{4,5},{5,4},{6,7},{7,6},{8,9},{9,8},{10,11... | collective-permute-start | bytes 393224 | tf_op jit(solution)/shard_map/ppermute | solution.py:324
  66.7 6.8 %collective-permute-start.5 = (bf16[4,128,128]{2,1,0:T(8,128)(2,1)S(1)}, bf16[4,128,128]{2,1,0:T(8,128)(2,1)S(1)}, u32[]{:S(2)}, u32[]{:S(2)}) collective-permute-start(bf16[4,128,128]{2,1,0:T(8,128)(2,1)S(1)} %pad_maximum_fusion.2), channel_id=1, source_target_pairs={{0,2},{1,3},{2,0},{3,1},{4,6},{5,7},{6,4},{7,5},{8,10},{9,11},{10,... | collective-permute-start | bytes 393224 | tf_op jit(solution)/shard_map/ppermute | solution.py:324
  69.3 5.5 %collective-permute-start.6 = (bf16[4,128,128]{2,1,0:T(8,128)(2,1)S(1)}, bf16[4,128,128]{2,1,0:T(8,128)(2,1)S(1)}, u32[]{:S(2)}, u32[]{:S(2)}) collective-permute-start(bf16[4,128,128]{2,1,0:T(8,128)(2,1)S(1)} %pad_maximum_fusion.3), channel_id=1, source_target_pairs={{0,3},{1,2},{2,1},{3,0},{4,7},{5,6},{6,5},{7,4},{8,11},{9,10},{10,... | collective-permute-start | bytes 393224 | tf_op jit(solution)/shard_map/ppermute | solution.py:324
  74.9 2.9 %copy-start = (bf16[8,512,512]{2,1,0:T(8,128)(2,1)S(1)}, bf16[8,512,512]{2,1,0:T(8,128)(2,1)}, u32[]{:S(2)}) copy-start(bf16[8,512,512]{2,1,0:T(8,128)(2,1)} %shard_map.84.weights_ref) | copy-start | bytes 12582916
  77.7 3.5 %collective-permute-start.8 = (bf16[2,2,8,2,64,128]{5,4,3,2,1,0:T(8,128)(2,1)S(1)}, bf16[2,2,8,2,64,128]{5,4,3,2,1,0:T(8,128)(2,1)S(1)}, u32[]{:S(2)}, u32[]{:S(2)}) collective-permute-start(bf16[2,2,8,2,64,128]{5,4,3,2,1,0:T(8,128)(2,1)S(1)} %get-tuple-element.24), channel_id=1, source_target_pairs={{0,32},{32,0},{1,33},{33,1},{2,34},{34,2},{3,35},{35,3},{4,36},{36... | collective-permute-start | bytes 3145736 | tf_op jit(solution)/shard_map/ppermute | solution.py:324
  80.6 5.3 %collective-permute-start.11 = (bf16[2,2,8,2,64,128]{5,4,3,2,1,0:T(8,128)(2,1)S(1)}, bf16[2,2,8,2,64,128]{5,4,3,2,1,0:T(8,128)(2,1)S(1)}, u32[]{:S(2)}, u32[]{:S(2)}) collective-permute-start(bf16[2,2,8,2,64,128]{5,4,3,2,1,0:T(8,128)(2,1)S(1)} %get-tuple-element.26), channel_id=1, source_target_pairs={{0,32},{32,0},{1,33},{33,1},{2,34},{34,2},{3,35},{35,3},{4,36},{36... | collective-permute-start | bytes 3145736 | tf_op jit(solution)/shard_map/ppermute | solution.py:324
  81.4 28.0 %collective-permute-start.9 = (bf16[2,8,2,64,128]{4,3,2,1,0:T(8,128)(2,1)S(1)}, bf16[2,8,2,64,128]{4,3,2,1,0:T(8,128)(2,1)S(1)}, u32[]{:S(2)}, u32[]{:S(2)}) collective-permute-start(bf16[2,8,2,64,128]{4,3,2,1,0:T(8,128)(2,1)S(1)} %fusion), channel_id=1, source_target_pairs={{0,128},{64,192},{128,0},{192,64},{1,129},{65,193},{129,1},{193,65... | collective-permute-start | bytes 1572872 | tf_op jit(solution)/shard_map/ppermute | solution.py:324
  85.9 38.2 %copy-start.2 = (bf16[2,256,256]{2,1,0:T(8,128)(2,1)S(1)}, bf16[2,256,256]{2,1,0:T(8,128)(2,1)}, u32[]{:S(2)}) copy-start(bf16[2,256,256]{2,1,0:T(8,128)(2,1)} %constant.32.clone.refs_8_) | copy-start | bytes 786436
  85.9 38.2 %copy-start.3 = (f32[16,128]{1,0:T(8,128)S(1)}, f32[16,128]{1,0:T(8,128)}, u32[]{:S(2)}) copy-start(f32[16,128]{1,0:T(8,128)} %constant.33.clone.refs_9_) | copy-start | bytes 24580
  86.1 23.7 %collective-permute-start.12 = (bf16[2,8,2,64,128]{4,3,2,1,0:T(8,128)(2,1)S(1)}, bf16[2,8,2,64,128]{4,3,2,1,0:T(8,128)(2,1)S(1)}, u32[]{:S(2)}, u32[]{:S(2)}) collective-permute-start(bf16[2,8,2,64,128]{4,3,2,1,0:T(8,128)(2,1)S(1)} %fusion.1), channel_id=1, source_target_pairs={{0,64},{64,0},{128,192},{192,128},{1,65},{65,1},{129,193},{193,129... | collective-permute-start | bytes 1572872 | tf_op jit(solution)/shard_map/ppermute | solution.py:324
  109.5 12.6 %collective-permute-start.10 = (bf16[8,2,64,128]{3,2,1,0:T(8,128)(2,1)S(1)}, bf16[8,2,64,128]{3,2,1,0:T(8,128)(2,1)S(1)}, u32[]{:S(2)}, u32[]{:S(2)}) collective-permute-start(bf16[8,2,64,128]{3,2,1,0:T(8,128)(2,1)S(1)} %fusion.3), channel_id=1, source_target_pairs={{0,64},{64,0},{128,192},{192,128},{1,65},{65,1},{129,193},{193,129... | collective-permute-start | bytes 786440 | tf_op jit(solution)/shard_map/ppermute | solution.py:324
  109.9 14.2 %collective-permute-start.13 = (bf16[8,2,64,128]{3,2,1,0:T(8,128)(2,1)S(1)}, bf16[8,2,64,128]{3,2,1,0:T(8,128)(2,1)S(1)}, u32[]{:S(2)}, u32[]{:S(2)}) collective-permute-start(bf16[8,2,64,128]{3,2,1,0:T(8,128)(2,1)S(1)} %fusion.2), channel_id=1, source_target_pairs={{0,128},{64,192},{128,0},{192,64},{1,129},{65,193},{129,1},{193,65... | collective-permute-start | bytes 786440 | tf_op jit(solution)/shard_map/ppermute | solution.py:324

commit v4 on v3

--- a/solution.py
+++ b/solution.py
@@ -65,7 +65,7 @@
 
 
 def channelize_kernel(
-    where_ref, volts_hbm, taper_ref, table_hbm, first_hbm, rest_hbm,
+    volts_hbm, taper_ref, table_hbm, first_hbm, rest_hbm,
     volts_ref, table_ref, frames_ref, turn_ref, first_ref, rest_ref, sems,
 ):
     blocks = SPECTRA // FIR_BLOCK
@@ -77,10 +77,11 @@
         copies.append(pltpu.make_async_copy(volts_hbm.at[:, span], volts_ref.at[:, span], sems.at[block]))
         copies[-1].start()
     table_copy = pltpu.make_async_copy(table_hbm, table_ref, sems.at[blocks])
-    table_copy.start()
 
     for block in range(blocks):
         copies[block].wait()
+        if block == 0:
+            table_copy.start()
 
         def fir_tile(nt, _, block=block):
             lane = pl.multiple_of(nt * LANES, LANES)
@@ -106,9 +107,10 @@
 
         lax.fori_loop(0, NT, fir_tile, 0)
     table_copy.wait()
-    far, near = 1 - where_ref[0], where_ref[0]
+    near = lax.axis_index("zh")
+    far, plane_id = 1 - near, 4 * lax.axis_index("y") + lax.axis_index("x")
     transform_block(table_ref[far, 0], frames_ref, turn_ref)
-    place(turn_ref, first_ref, where_ref[1])
+    place(turn_ref, first_ref, plane_id)
     copies = [pltpu.make_async_copy(first_ref, first_hbm, sems.at[blocks + 1])]
     copies[0].start()
     sent = first_ref.shape[1]
@@ -124,7 +126,7 @@
         copy.wait()
 
 
-def channelize(where, volts, table):
+def channelize(volts, table):
     taper = jnp.asarray(np.broadcast_to(taper_table()[:, None, :], (TAPS, OWN, NFFT)).copy())
     sent = table.shape[2] * OWN // PLANE
     first = jax.ShapeDtypeStruct((PLANE, sent, SPECTRA), jnp.bfloat16)
@@ -133,7 +135,7 @@
     return pl.pallas_call(
         channelize_kernel,
         out_shape=(first, rest),
-        in_specs=[pl.BlockSpec(memory_space=pltpu.SMEM), hbm, vmem, hbm],
+        in_specs=[hbm, vmem, hbm],
         out_specs=(hbm, hbm),
         scratch_shapes=[
             pltpu.VMEM(volts.shape, jnp.bfloat16),
@@ -146,7 +148,7 @@
         ],
         compiler_params=pltpu.CompilerParams(vmem_limit_bytes=LARGE),
         cost_estimate=SHORT,
-    )(where, volts, taper, table)
+    )(volts, taper, table)
 
 
 def one_hot(rows, columns):
@@ -361,7 +363,7 @@
         value = lax.all_to_all(value.reshape(PLANE, -1, SPECTRA), ("y", "x"), split_axis=0, concat_axis=0, tiled=True)
         return value.reshape(PLANE, -1, 2 * OWN, SPECTRA)
 
-    first, rest = channelize(where, voltages, table)
+    first, rest = channelize(voltages, table)
     far0 = swap(first, "zh", 1, 2)
     planed = turn(rest)
     far1 = swap(planed[:, :half], "zh", 1, 2)

time: 127 us -> 126 us (level)
  no operation moved by 1% of the time
where the time goes in v4:
time: 126 us
  waiting for transfers between devices  43.9 us (35%)
  starting transfers between devices  41.9 us (33%)
  Pallas kernels  38.3 us (30%)
  other arithmetic  1.26 us (1%)
    ppermute x14, waiting for transfers between devices, swap(): return lax.ppermute(value, axis, [(k, k ^ distance) for k in range(size)])  43.9 us
    ppermute x14, starting transfers between devices, swap(): return lax.ppermute(value, axis, [(k, k ^ distance) for k in range(size)])  34.3 us
    pallas_call x2, Pallas kernels, arrange_weights(): pl.pallas_call(functools.partial(weight_kernel, chunk == 0), grid_spec=pl...  18.1 us
    pallas_call x1, Pallas kernels, channelize(): pl.pallas_call(channelize_kernel, out_shape=(first, rest), in_specs=[hbm,...  12.4 us
    all_to_all x1, starting transfers between devices, turn(): lax.all_to_all(value.reshape(PLANE, -1, SPECTRA), ('y', 'x'), split_axis=...  7.62 us
    pallas_call x2, Pallas kernels, combine(): pl.pallas_call(functools.partial(combine_kernel, chunk == 1), grid=(chans...  5.61 us
  transfers between devices with their start and end apart: 15, of which 10 were waited for; matrix products, arithmetic and copies ran while one was open for 1% of the time, Pallas kernels for 17%

profile of v4, /device:TPU:2, one launch (start us, length us, event | category | flops | bytes accessed | tf_op | source)
XLA Modules:
  0.0 125.6 jit_solution(14306107398994826622)
XLA Ops:
  0.0 12.4 %shard_map.82 = (bf16[16,128,128]{2,1,0:T(8,128)(2,1)}, bf16[16,384,128]{2,1,0:T(8,128)(2,1)}) custom-call(bf16[8,268288]{1,0:T(8,128)(2,1)} %volts_hbm.1, f32[4,8,2048]{2,1,0:T(8,128)} %constant.31.clone.taper_ref, bf16[2,2,256,2048]{3,2,1,0:T(8,128)(2,1)} %constant.30.clone.table_hbm), custom_call_target="tpu_custom_call" | custom-call | flops 1 | bytes 1 | tf_op jit(solution)/shard_map/pallas_call | solution.py:135
  12.4 0.0 copy-start.4
  12.4 7.6 %all-to-all-start = ((bf16[16,384,128]{2,1,0:T(8,128)(2,1)}), bf16[16,384,128]{2,1,0:T(8,128)(2,1)S(1)}, u32[]{:S(2)}, u32[]{:S(2)}) async-start(bf16[16,384,128]{2,1,0:T(8,128)(2,1)} %get-tuple-element.16), calls=%async_computation | async-start | bytes 3145728 | tf_op jit(solution)/shard_map/all_to_all | solution.py:363
  20.1 0.0 copy-done.4
  20.1 7.3 %collective-permute-start = (bf16[16,128,128]{2,1,0:T(8,128)(2,1)S(1)}, bf16[16,128,128]{2,1,0:T(8,128)(2,1)S(1)}, u32[]{:S(2)}, u32[]{:S(2)}) collective-permute-start(bf16[16,128,128]{2,1,0:T(8,128)(2,1)S(1)} %copy-done.4), channel_id=1, source_target_pairs={{0,4},{4,0},{1,5},{5,1},{2,6},{6,2},{3,7},{7,3},{8,12},{12,8},{9,1... | collective-permute-start | bytes 1572872 | tf_op jit(solution)/shard_map/ppermute | solution.py:326
  27.3 0.6 pad_add_fusion.where_ref
  27.9 9.0 %shard_map.83.weights_ref = bf16[8,512,512]{2,1,0:T(8,128)(2,1)} custom-call(s32[4]{0:T(128)} %pad_add_fusion.where_ref, s32[1,512]{1,0:T(1,128)} %bitcast.38, s32[1,256]{1,0:T(1,128)} %bitcast.40, bf16[16,2,512,256]{3,2,1,0:T(8,128)(2,1)} %weights_ref.1), custom_call_target="tpu_custom_call" | custom-call | flops 1 | bytes 1 | tf_op jit(solution)/shard_map/pallas_call | solution.py:204
  36.9 9.1 %shard_map.84.weights_ref = bf16[8,512,512]{2,1,0:T(8,128)(2,1)} custom-call(s32[4]{0:T(128)} %pad_add_fusion.where_ref, s32[1,512]{1,0:T(1,128)} %bitcast.39, s32[1,256]{1,0:T(1,128)} %bitcast.41, bf16[16,2,512,256]{3,2,1,0:T(8,128)(2,1)} %weights_ref.1), custom_call_target="tpu_custom_call" | custom-call | flops 1 | bytes 1 | tf_op jit(solution)/shard_map/pallas_call | solution.py:204
  46.0 0.0 collective-permute-done
  46.0 0.0 all-to-all-done
  46.0 0.0 copy-start.1
  46.1 9.1 %collective-permute-start.7 = (bf16[16,8,16,128]{3,2,1,0:T(8,128)(2,1)S(1)}, bf16[16,8,16,128]{3,2,1,0:T(8,128)(2,1)S(1)}, u32[]{:S(2)}, u32[]{:S(2)}) collective-permute-start(bf16[16,8,16,128]{3,2,1,0:T(8,128)(2,1)S(1)} %slice.142), channel_id=1, source_target_pairs={{0,4},{4,0},{1,5},{5,1},{2,6},{6,2},{3,7},{7,3},{8,12},{12,8},{9,1... | collective-permute-start | bytes 1572872 | tf_op jit(solution)/shard_map/ppermute | solution.py:326
  55.3 1.6 %collective-permute-start.1 = (bf16[4,128,128]{2,1,0:T(8,128)(2,1)S(1)}, bf16[4,128,128]{2,1,0:T(8,128)(2,1)S(1)}, u32[]{:S(2)}, u32[]{:S(2)}) collective-permute-start(bf16[4,128,128]{2,1,0:T(8,128)(2,1)S(1)} %get-tuple-element.31), channel_id=1, source_target_pairs={{0,8},{8,0},{16,24},{24,16},{1,9},{9,1},{17,25},{25,17},{2,10},{10... | collective-permute-start | bytes 393224 | tf_op jit(solution)/shard_map/ppermute | solution.py:326
  56.8 2.1 %collective-permute-start.3 = (bf16[4,128,128]{2,1,0:T(8,128)(2,1)S(1)}, bf16[4,128,128]{2,1,0:T(8,128)(2,1)S(1)}, u32[]{:S(2)}, u32[]{:S(2)}) collective-permute-start(bf16[4,128,128]{2,1,0:T(8,128)(2,1)S(1)} %get-tuple-element.32), channel_id=1, source_target_pairs={{0,24},{8,16},{16,8},{24,0},{1,25},{9,17},{17,9},{25,1},{2,26},{10... | collective-permute-start | bytes 393224 | tf_op jit(solution)/shard_map/ppermute | solution.py:326
  58.9 0.6 collective-permute-start.2
  59.5 0.8 collective-permute-done.1
  60.3 2.7 %collective-permute-done.3 = bf16[4,128,128]{2,1,0:T(8,128)(2,1)S(1)} collective-permute-done((bf16[4,128,128]{2,1,0:T(8,128)(2,1)S(1)}, bf16[4,128,128]{2,1,0:T(8,128)(2,1)S(1)}, u32[]{:S(2)}, u32[]{:S(2)}) %collective-permute-start.3) | collective-permute-done | bytes 131104 | tf_op jit(solution)/shard_map/ppermute | solution.py:326
  63.0 2.4 %collective-permute-done.2 = bf16[4,128,128]{2,1,0:T(8,128)(2,1)S(1)} collective-permute-done((bf16[4,128,128]{2,1,0:T(8,128)(2,1)S(1)}, bf16[4,128,128]{2,1,0:T(8,128)(2,1)S(1)}, u32[]{:S(2)}, u32[]{:S(2)}) %collective-permute-start.2) | collective-permute-done | bytes 131104 | tf_op jit(solution)/shard_map/ppermute | solution.py:326
  65.4 0.6 collective-permute-start.4
  66.1 2.6 %collective-permute-start.5 = (bf16[4,128,128]{2,1,0:T(8,128)(2,1)S(1)}, bf16[4,128,128]{2,1,0:T(8,128)(2,1)S(1)}, u32[]{:S(2)}, u32[]{:S(2)}) collective-permute-start(bf16[4,128,128]{2,1,0:T(8,128)(2,1)S(1)} %pad_maximum_fusion.2), channel_id=1, source_target_pairs={{0,2},{1,3},{2,0},{3,1},{4,6},{5,7},{6,4},{7,5},{8,10},{9,11},{10,... | collective-permute-start | bytes 393224 | tf_op jit(solution)/shard_map/ppermute | solution.py:326
  68.7 0.7 collective-permute-start.6
  69.4 1.1 collective-permute-done.4
  70.4 2.4 %collective-permute-done.5 = bf16[4,128,128]{2,1,0:T(8,128)(2,1)S(1)} collective-permute-done((bf16[4,128,128]{2,1,0:T(8,128)(2,1)S(1)}, bf16[4,128,128]{2,1,0:T(8,128)(2,1)S(1)}, u32[]{:S(2)}, u32[]{:S(2)}) %collective-permute-start.5) | collective-permute-done | bytes 131104 | tf_op jit(solution)/shard_map/ppermute | solution.py:326
  72.8 1.4 %collective-permute-done.6 = bf16[4,128,128]{2,1,0:T(8,128)(2,1)S(1)} collective-permute-done((bf16[4,128,128]{2,1,0:T(8,128)(2,1)S(1)}, bf16[4,128,128]{2,1,0:T(8,128)(2,1)S(1)}, u32[]{:S(2)}, u32[]{:S(2)}) %collective-permute-start.6) | collective-permute-done | bytes 131104 | tf_op jit(solution)/shard_map/ppermute | solution.py:326
  74.2 0.1 pad_maximum_fusion
  74.3 0.0 collective-permute-done.7.far_ref
  74.3 0.0 copy-done.1
  74.3 0.0 copy-start
  74.3 2.8 %shard_map.85 = (f32[2,2,8,2,64,128]{5,4,3,2,1,0:T(8,128)S(1)}, bf16[2,2,8,2,64,128]{5,4,3,2,1,0:T(8,128)(2,1)S(1)}) custom-call(bf16[8,512,512]{2,1,0:T(8,128)(2,1)S(1)} %copy-done.1, bf16[16,24,16,128]{3,2,1,0:T(8,128)(2,1)S(1)} %bitcast.32, bf16[16,8,16,128]{3,2,1,0:T(8,128)(2,1)S(1)} %bitcast.34), custom_call_target="tpu_custom_call" | custom-call | flops 1 | bytes 1 | tf_op jit(solution)/shard_map/pallas_call | solution.py:251
  77.1 0.1 collective-permute-start.8
  77.2 0.0 copy-done
  77.2 2.8 %shard_map.86 = (f32[2,2,8,2,64,128]{5,4,3,2,1,0:T(8,128)S(1)}, bf16[2,2,8,2,64,128]{5,4,3,2,1,0:T(8,128)(2,1)S(1)}) custom-call(bf16[8,512,512]{2,1,0:T(8,128)(2,1)S(1)} %copy-done, bf16[16,24,16,128]{3,2,1,0:T(8,128)(2,1)S(1)} %bitcast.33, bf16[16,8,16,128]{3,2,1,0:T(8,128)(2,1)S(1)} %collective-permute-done.7.far_ref), custom_call_target="tpu_custom_call" | custom-call | flops 1 | bytes 1 | tf_op jit(solution)/shard_map/pallas_call | solution.py:251
  80.0 0.6 collective-permute-start.11
  80.6 0.0 collective-permute-done.8.refs_1_
  80.6 0.2 fusion
  80.8 4.6 %collective-permute-start.9 = (bf16[2,8,2,64,128]{4,3,2,1,0:T(8,128)(2,1)S(1)}, bf16[2,8,2,64,128]{4,3,2,1,0:T(8,128)(2,1)S(1)}, u32[]{:S(2)}, u32[]{:S(2)}) collective-permute-start(bf16[2,8,2,64,128]{4,3,2,1,0:T(8,128)(2,1)S(1)} %fusion), channel_id=1, source_target_pairs={{0,128},{64,192},{128,0},{192,64},{1,129},{65,193},{129,1},{193,65... | collective-permute-start | bytes 1572872 | tf_op jit(solution)/shard_map/ppermute | solution.py:326
  85.4 0.0 collective-permute-done.11.refs_5_
  85.4 0.0 copy-start.2
  85.4 0.0 copy-start.3
  85.4 0.2 fusion.1
  85.5 1.8 %collective-permute-start.12 = (bf16[2,8,2,64,128]{4,3,2,1,0:T(8,128)(2,1)S(1)}, bf16[2,8,2,64,128]{4,3,2,1,0:T(8,128)(2,1)S(1)}, u32[]{:S(2)}, u32[]{:S(2)}) collective-permute-start(bf16[2,8,2,64,128]{4,3,2,1,0:T(8,128)(2,1)S(1)} %fusion.1), channel_id=1, source_target_pairs={{0,64},{64,0},{128,192},{192,128},{1,65},{65,1},{129,193},{193,129... | collective-permute-start | bytes 1572872 | tf_op jit(solution)/shard_map/ppermute | solution.py:326
  87.3 21.5 %collective-permute-done.9.refs_2_ = bf16[2,8,2,64,128]{4,3,2,1,0:T(8,128)(2,1)S(1)} collective-permute-done((bf16[2,8,2,64,128]{4,3,2,1,0:T(8,128)(2,1)S(1)}, bf16[2,8,2,64,128]{4,3,2,1,0:T(8,128)(2,1)S(1)}, u32[]{:S(2)}, u32[]{:S(2)}) %collective-permute-start.9) | collective-permute-done | bytes 524320 | tf_op jit(solution)/shard_map/ppermute | solution.py:326
  108.8 0.1 fusion.3
  108.9 0.1 collective-permute-start.10
  109.0 0.1 collective-permute-done.12.refs_6_
  109.2 0.1 fusion.2
  109.3 2.6 %collective-permute-start.13 = (bf16[8,2,64,128]{3,2,1,0:T(8,128)(2,1)S(1)}, bf16[8,2,64,128]{3,2,1,0:T(8,128)(2,1)S(1)}, u32[]{:S(2)}, u32[]{:S(2)}) collective-permute-start(bf16[8,2,64,128]{3,2,1,0:T(8,128)(2,1)S(1)} %fusion.2), channel_id=1, source_target_pairs={{0,128},{64,192},{128,0},{192,64},{1,129},{65,193},{129,1},{193,65... | collective-permute-start | bytes 786440 | tf_op jit(solution)/shard_map/ppermute | solution.py:326
  111.8 9.7 %collective-permute-done.10.refs_3_ = bf16[8,2,64,128]{3,2,1,0:T(8,128)(2,1)S(1)} collective-permute-done((bf16[8,2,64,128]{3,2,1,0:T(8,128)(2,1)S(1)}, bf16[8,2,64,128]{3,2,1,0:T(8,128)(2,1)S(1)}, u32[]{:S(2)}, u32[]{:S(2)}) %collective-permute-start.10) | collective-permute-done | bytes 262176 | tf_op jit(solution)/shard_map/ppermute | solution.py:326
  121.6 1.9 %collective-permute-done.13.refs_7_ = bf16[8,2,64,128]{3,2,1,0:T(8,128)(2,1)S(1)} collective-permute-done((bf16[8,2,64,128]{3,2,1,0:T(8,128)(2,1)S(1)}, bf16[8,2,64,128]{3,2,1,0:T(8,128)(2,1)S(1)}, u32[]{:S(2)}, u32[]{:S(2)}) %collective-permute-start.13) | collective-permute-done | bytes 262176 | tf_op jit(solution)/shard_map/ppermute | solution.py:326
  123.5 0.0 copy-done.2
  123.5 0.0 copy-done.3
  123.5 2.1 %shard_map.87 = f32[16,16,64]{2,1,0:T(8,128)} custom-call(f32[2,2,8,2,64,128]{5,4,3,2,1,0:T(8,128)S(1)} %get-tuple-element.23.refs_0_, bf16[2,2,8,2,64,128]{5,4,3,2,1,0:T(8,128)(2,1)S(1)} %collective-permute-done.8.refs_1_, bf16[2,8,2,64,128]{4,3,2,1,0:T(8,128)(2,1)S(1)} %collective-permute-done.9.refs_2_, ...), custom_call_target="tpu_custom_call" | custom-call | flops 1 | bytes 1 | tf_op jit(solution)/shard_map/pallas_call | solution.py:314
  (10 shorter events, 0.2 us)
Async XLA Ops:
  12.4 7.6 %copy-start.4 = (bf16[16,128,128]{2,1,0:T(8,128)(2,1)S(1)}, bf16[16,128,128]{2,1,0:T(8,128)(2,1)}, u32[]{:S(2)}) copy-start(bf16[16,128,128]{2,1,0:T(8,128)(2,1)} %get-tuple-element.18) | copy-start | bytes 1572868
  12.4 33.6 %all-to-all-start = ((bf16[16,384,128]{2,1,0:T(8,128)(2,1)}), bf16[16,384,128]{2,1,0:T(8,128)(2,1)S(1)}, u32[]{:S(2)}, u32[]{:S(2)}) async-start(bf16[16,384,128]{2,1,0:T(8,128)(2,1)} %get-tuple-element.16), calls=%async_computation | async-start | bytes 3145728 | tf_op jit(solution)/shard_map/all_to_all | solution.py:363
  20.1 25.9 %collective-permute-start = (bf16[16,128,128]{2,1,0:T(8,128)(2,1)S(1)}, bf16[16,128,128]{2,1,0:T(8,128)(2,1)S(1)}, u32[]{:S(2)}, u32[]{:S(2)}) collective-permute-start(bf16[16,128,128]{2,1,0:T(8,128)(2,1)S(1)} %copy-done.4), channel_id=1, source_target_pairs={{0,4},{4,0},{1,5},{5,1},{2,6},{6,2},{3,7},{7,3},{8,12},{12,8},{9,1... | collective-permute-start | bytes 1572872 | tf_op jit(solution)/shard_map/ppermute | solution.py:326
  46.0 28.3 %copy-start.1 = (bf16[8,512,512]{2,1,0:T(8,128)(2,1)S(1)}, bf16[8,512,512]{2,1,0:T(8,128)(2,1)}, u32[]{:S(2)}) copy-start(bf16[8,512,512]{2,1,0:T(8,128)(2,1)} %shard_map.83.weights_ref) | copy-start | bytes 12582916
  46.1 28.2 %collective-permute-start.7 = (bf16[16,8,16,128]{3,2,1,0:T(8,128)(2,1)S(1)}, bf16[16,8,16,128]{3,2,1,0:T(8,128)(2,1)S(1)}, u32[]{:S(2)}, u32[]{:S(2)}) collective-permute-start(bf16[16,8,16,128]{3,2,1,0:T(8,128)(2,1)S(1)} %slice.142), channel_id=1, source_target_pairs={{0,4},{4,0},{1,5},{5,1},{2,6},{6,2},{3,7},{7,3},{8,12},{12,8},{9,1... | collective-permute-start | bytes 1572872 | tf_op jit(solution)/shard_map/ppermute | solution.py:326
  55.3 5.1 %collective-permute-start.1 = (bf16[4,128,128]{2,1,0:T(8,128)(2,1)S(1)}, bf16[4,128,128]{2,1,0:T(8,128)(2,1)S(1)}, u32[]{:S(2)}, u32[]{:S(2)}) collective-permute-start(bf16[4,128,128]{2,1,0:T(8,128)(2,1)S(1)} %get-tuple-element.31), channel_id=1, source_target_pairs={{0,8},{8,0},{16,24},{24,16},{1,9},{9,1},{17,25},{25,17},{2,10},{10... | collective-permute-start | bytes 393224 | tf_op jit(solution)/shard_map/ppermute | solution.py:326
  56.8 6.2 %collective-permute-start.3 = (bf16[4,128,128]{2,1,0:T(8,128)(2,1)S(1)}, bf16[4,128,128]{2,1,0:T(8,128)(2,1)S(1)}, u32[]{:S(2)}, u32[]{:S(2)}) collective-permute-start(bf16[4,128,128]{2,1,0:T(8,128)(2,1)S(1)} %get-tuple-element.32), channel_id=1, source_target_pairs={{0,24},{8,16},{16,8},{24,0},{1,25},{9,17},{17,9},{25,1},{2,26},{10... | collective-permute-start | bytes 393224 | tf_op jit(solution)/shard_map/ppermute | solution.py:326
  58.9 6.5 %collective-permute-start.2 = (bf16[4,128,128]{2,1,0:T(8,128)(2,1)S(1)}, bf16[4,128,128]{2,1,0:T(8,128)(2,1)S(1)}, u32[]{:S(2)}, u32[]{:S(2)}) collective-permute-start(bf16[4,128,128]{2,1,0:T(8,128)(2,1)S(1)} %get-tuple-element.33), channel_id=1, source_target_pairs={{0,16},{8,24},{16,0},{24,8},{1,17},{9,25},{17,1},{25,9},{2,18},{10... | collective-permute-start | bytes 393224 | tf_op jit(solution)/shard_map/ppermute | solution.py:326
  65.4 5.1 %collective-permute-start.4 = (bf16[4,128,128]{2,1,0:T(8,128)(2,1)S(1)}, bf16[4,128,128]{2,1,0:T(8,128)(2,1)S(1)}, u32[]{:S(2)}, u32[]{:S(2)}) collective-permute-start(bf16[4,128,128]{2,1,0:T(8,128)(2,1)S(1)} %pad_maximum_fusion.1), channel_id=1, source_target_pairs={{0,1},{1,0},{2,3},{3,2},{4,5},{5,4},{6,7},{7,6},{8,9},{9,8},{10,11... | collective-permute-start | bytes 393224 | tf_op jit(solution)/shard_map/ppermute | solution.py:326
  66.1 6.8 %collective-permute-start.5 = (bf16[4,128,128]{2,1,0:T(8,128)(2,1)S(1)}, bf16[4,128,128]{2,1,0:T(8,128)(2,1)S(1)}, u32[]{:S(2)}, u32[]{:S(2)}) collective-permute-start(bf16[4,128,128]{2,1,0:T(8,128)(2,1)S(1)} %pad_maximum_fusion.2), channel_id=1, source_target_pairs={{0,2},{1,3},{2,0},{3,1},{4,6},{5,7},{6,4},{7,5},{8,10},{9,11},{10,... | collective-permute-start | bytes 393224 | tf_op jit(solution)/shard_map/ppermute | solution.py:326
  68.7 5.5 %collective-permute-start.6 = (bf16[4,128,128]{2,1,0:T(8,128)(2,1)S(1)}, bf16[4,128,128]{2,1,0:T(8,128)(2,1)S(1)}, u32[]{:S(2)}, u32[]{:S(2)}) collective-permute-start(bf16[4,128,128]{2,1,0:T(8,128)(2,1)S(1)} %pad_maximum_fusion.3), channel_id=1, source_target_pairs={{0,3},{1,2},{2,1},{3,0},{4,7},{5,6},{6,5},{7,4},{8,11},{9,10},{10,... | collective-permute-start | bytes 393224 | tf_op jit(solution)/shard_map/ppermute | solution.py:326
  74.3 2.9 %copy-start = (bf16[8,512,512]{2,1,0:T(8,128)(2,1)S(1)}, bf16[8,512,512]{2,1,0:T(8,128)(2,1)}, u32[]{:S(2)}) copy-start(bf16[8,512,512]{2,1,0:T(8,128)(2,1)} %shard_map.84.weights_ref) | copy-start | bytes 12582916
  77.1 3.5 %collective-permute-start.8 = (bf16[2,2,8,2,64,128]{5,4,3,2,1,0:T(8,128)(2,1)S(1)}, bf16[2,2,8,2,64,128]{5,4,3,2,1,0:T(8,128)(2,1)S(1)}, u32[]{:S(2)}, u32[]{:S(2)}) collective-permute-start(bf16[2,2,8,2,64,128]{5,4,3,2,1,0:T(8,128)(2,1)S(1)} %get-tuple-element.24), channel_id=1, source_target_pairs={{0,32},{32,0},{1,33},{33,1},{2,34},{34,2},{3,35},{35,3},{4,36},{36... | collective-permute-start | bytes 3145736 | tf_op jit(solution)/shard_map/ppermute | solution.py:326
  80.0 5.3 %collective-permute-start.11 = (bf16[2,2,8,2,64,128]{5,4,3,2,1,0:T(8,128)(2,1)S(1)}, bf16[2,2,8,2,64,128]{5,4,3,2,1,0:T(8,128)(2,1)S(1)}, u32[]{:S(2)}, u32[]{:S(2)}) collective-permute-start(bf16[2,2,8,2,64,128]{5,4,3,2,1,0:T(8,128)(2,1)S(1)} %get-tuple-element.26), channel_id=1, source_target_pairs={{0,32},{32,0},{1,33},{33,1},{2,34},{34,2},{3,35},{35,3},{4,36},{36... | collective-permute-start | bytes 3145736 | tf_op jit(solution)/shard_map/ppermute | solution.py:326
  80.8 28.0 %collective-permute-start.9 = (bf16[2,8,2,64,128]{4,3,2,1,0:T(8,128)(2,1)S(1)}, bf16[2,8,2,64,128]{4,3,2,1,0:T(8,128)(2,1)S(1)}, u32[]{:S(2)}, u32[]{:S(2)}) collective-permute-start(bf16[2,8,2,64,128]{4,3,2,1,0:T(8,128)(2,1)S(1)} %fusion), channel_id=1, source_target_pairs={{0,128},{64,192},{128,0},{192,64},{1,129},{65,193},{129,1},{193,65... | collective-permute-start | bytes 1572872 | tf_op jit(solution)/shard_map/ppermute | solution.py:326
  85.4 38.1 %copy-start.2 = (bf16[2,256,256]{2,1,0:T(8,128)(2,1)S(1)}, bf16[2,256,256]{2,1,0:T(8,128)(2,1)}, u32[]{:S(2)}) copy-start(bf16[2,256,256]{2,1,0:T(8,128)(2,1)} %constant.32.clone.refs_8_) | copy-start | bytes 786436
  85.4 38.1 %copy-start.3 = (f32[16,128]{1,0:T(8,128)S(1)}, f32[16,128]{1,0:T(8,128)}, u32[]{:S(2)}) copy-start(f32[16,128]{1,0:T(8,128)} %constant.33.clone.refs_9_) | copy-start | bytes 24580
  85.5 23.6 %collective-permute-start.12 = (bf16[2,8,2,64,128]{4,3,2,1,0:T(8,128)(2,1)S(1)}, bf16[2,8,2,64,128]{4,3,2,1,0:T(8,128)(2,1)S(1)}, u32[]{:S(2)}, u32[]{:S(2)}) collective-permute-start(bf16[2,8,2,64,128]{4,3,2,1,0:T(8,128)(2,1)S(1)} %fusion.1), channel_id=1, source_target_pairs={{0,64},{64,0},{128,192},{192,128},{1,65},{65,1},{129,193},{193,129... | collective-permute-start | bytes 1572872 | tf_op jit(solution)/shard_map/ppermute | solution.py:326
  108.9 12.6 %collective-permute-start.10 = (bf16[8,2,64,128]{3,2,1,0:T(8,128)(2,1)S(1)}, bf16[8,2,64,128]{3,2,1,0:T(8,128)(2,1)S(1)}, u32[]{:S(2)}, u32[]{:S(2)}) collective-permute-start(bf16[8,2,64,128]{3,2,1,0:T(8,128)(2,1)S(1)} %fusion.3), channel_id=1, source_target_pairs={{0,64},{64,0},{128,192},{192,128},{1,65},{65,1},{129,193},{193,129... | collective-permute-start | bytes 786440 | tf_op jit(solution)/shard_map/ppermute | solution.py:326
  109.3 14.2 %collective-permute-start.13 = (bf16[8,2,64,128]{3,2,1,0:T(8,128)(2,1)S(1)}, bf16[8,2,64,128]{3,2,1,0:T(8,128)(2,1)S(1)}, u32[]{:S(2)}, u32[]{:S(2)}) collective-permute-start(bf16[8,2,64,128]{3,2,1,0:T(8,128)(2,1)S(1)} %fusion.2), channel_id=1, source_target_pairs={{0,128},{64,192},{128,0},{192,64},{1,129},{65,193},{129,1},{193,65... | collective-permute-start | bytes 786440 | tf_op jit(solution)/shard_map/ppermute | solution.py:326
